TPU v7x, 32 devices: a whole 2x2x4 slice. The times are simulated.
32 devices in a mesh: row: 4 (over y, x), col: 8 (over z, core).
Axes of the slice: x: 2, y: 2, z: 4, core: 2. Of those that a mesh axis runs over, the one named last changes fastest.
Arguments:
- base_input: bfloat16 [1024, 16384], P('col', 'row'), may hold values from -6 to 6
- layer_input: bfloat16 [1024, 16384], P('row', 'col'), may hold values from -6 to 6
- out_grad: bfloat16 [1024, 16384], P('col', 'row'), may hold values from -6 to 6
- cross_weight: bfloat16 [16384, 16384], P('row', 'col'), may hold values from -0.046875 to 0.046875
- cross_bias: bfloat16 [16384], P('row'), may hold values from -5 to 5
Outputs:
- weight_grad: float32 [16384, 16384], P('row', 'col')
- bias_grad: float32 [16384], P('row')
- base_grad: bfloat16 [1024, 16384], P('col', 'row')
- branch_grad: bfloat16 [1024, 16384], P('row', 'col')
All inputs are finite; a program needn't handle non-finite values.
Results may differ from a plain program's by a relative error of at most 0.019.
Values may be sent and summed in bfloat16 or wider, within the bound.
No kernel may reach another device: no remote copies, remote signals or barrier semaphores. Data moves between devices by JAX's collectives and lax.ppermute only.
A program may use at most 128 MiB of HBM per device.

v0:
```python
import jax
import jax.numpy as jnp
from jax import lax
from jax.sharding import PartitionSpec as P


def on_device(base_input, layer_input, out_grad, cross_weight, cross_bias):
    input_panel = lax.all_gather(layer_input, "row", axis=0, tiled=True)
    grad_panel, base_panel = (
        lax.all_gather(out_grad, "col", axis=0, tiled=True),
        lax.all_gather(base_input, "col", axis=0, tiled=True),
    )
    hidden_panel = (grad_panel.astype(jnp.float32) * base_panel.astype(jnp.float32)).astype(
        jnp.bfloat16
    )
    weight_grad = lax.dot_general(
        hidden_panel, input_panel, (((0,), (0,)), ((), ())), preferred_element_type=jnp.float32
    )
    bias_grad = jnp.sum(hidden_panel, axis=0, dtype=jnp.float32)
    rows = input_panel
    preact = lax.psum_scatter(
        lax.dot_general(
            rows, cross_weight, (((1,), (1,)), ((), ())), preferred_element_type=jnp.float32
        ).astype(jnp.bfloat16),
        "col",
        scatter_dimension=0,
        tiled=True,
    ).astype(jnp.float32)
    preact = preact + cross_bias.astype(jnp.float32)[None, :]
    base_grad = (out_grad.astype(jnp.float32) * preact).astype(jnp.bfloat16)
    rows = hidden_panel
    branch = lax.psum_scatter(
        jnp.dot(rows, cross_weight, preferred_element_type=jnp.float32).astype(jnp.bfloat16),
        "row",
        scatter_dimension=0,
        tiled=True,
    )
    return (weight_grad, bias_grad, base_grad, branch)


def solution(mesh):
    in_specs = (P("col", "row"), P("row", "col"), P("col", "row"), P("row", "col"), P("row"))
    out_specs = (P("row", "col"), P("row"), P("col", "row"), P("row", "col"))
    return jax.shard_map(
        on_device, mesh=mesh, in_specs=in_specs, out_specs=out_specs, check_vma=False
    )
```

profile of v0, /device:TPU:0, one launch (start us, length us, event | category | flops | bytes accessed | tf_op | source)
XLA Modules:
  0.0 382.5 jit_solution(11118763317831707011)
XLA Ops:
  7.2 0.0 all-gather.8.cloned.1.call-start
  7.2 0.7 all-gather.8.cloned.1.call-update
  7.9 0.0 all-gather.6.cloned.1.call-start
  7.9 0.7 all-gather.6.cloned.1.call-update
  8.6 0.0 all-gather.4.cloned.1.call-start
  8.7 0.7 all-gather.4.cloned.1.call-update
  9.4 0.0 reduce-scatter.3.cloned.1.call-start
  9.4 55.9 %all-gather.8.cloned.1.call-done = bf16[1024,2048]{1,0:T(8,128)(2,1)} async-done(((bf16[256,2048]{1,0:T(8,128)(2,1)}), bf16[1024,2048]{1,0:T(8,128)(2,1)}) %all-gather.8.cloned.1.call-update) | async-done | bytes 4194320 | tf_op jit(solution)/shard_map/all_gather | solution.py:8
  65.3 23.0 %convolution_convert_fusion = bf16[1024,4096]{1,0:T(8,128)(2,1)} fusion(bf16[1024,2048]{1,0:T(8,128)(2,1)} %all-gather.8.cloned.1.call-done, bf16[4096,2048]{1,0:T(8,128)(2,1)} %param.8), kind=kOutput, calls=%fused_computation.2 | convolution fusion | flops 17184063488 | bytes 29360128 | tf_op jit(solution)/shard_map/dot_general | solution.py:22
  88.3 0.0 reduce-scatter.3.cloned.1.call-update
  88.3 0.0 copy-start.1
  88.3 0.0 reduce-scatter.5.cloned.1.call-start
  88.4 60.6 %all-gather.6.cloned.1.call-done = bf16[1024,4096]{1,0:T(8,128)(2,1)} async-done(((bf16[128,4096]{1,0:T(8,128)(2,1)}), bf16[1024,4096]{1,0:T(8,128)(2,1)}) %all-gather.6.cloned.1.call-update) | async-done | bytes 8388624 | tf_op jit(solution)/shard_map/all_gather | solution.py:11
  149.0 82.2 %all-gather.4.cloned.1.call-done = bf16[1024,4096]{1,0:T(8,128)(2,1)} async-done(((bf16[128,4096]{1,0:T(8,128)(2,1)}), bf16[1024,4096]{1,0:T(8,128)(2,1)}) %all-gather.4.cloned.1.call-update) | async-done | bytes 8388624 | tf_op jit(solution)/shard_map/all_gather | solution.py:10
  231.2 26.4 %convolution_convert_fusion.1 = bf16[1024,2048]{1,0:T(8,128)(2,1)} fusion(bf16[4096,2048]{1,0:T(8,128)(2,1)} %param.8, bf16[1024,4096]{1,0:T(8,128)(2,1)} %all-gather.6.cloned.1.call-done, bf16[1024,4096]{1,0:T(8,128)(2,1)} %all-gather.4.cloned.1.call-done), kind=kOutput, calls=%fused_computation.3 | convolution fusion | flops 17198743552 | bytes 37748736 | tf_op jit(solution)/shard_map/dot_general | solution.py:33
  257.6 0.0 reduce-scatter.5.cloned.1.call-update
  257.6 0.0 copy-done.1
  257.7 10.0 %convert_reduce_fusion = f32[4096]{0:T(1024)} fusion(bf16[1024,4096]{1,0:T(8,128)(2,1)} %all-gather.6.cloned.1.call-done, bf16[1024,4096]{1,0:T(8,128)(2,1)} %all-gather.4.cloned.1.call-done), kind=kLoop, calls=%fused_computation | loop fusion | flops 25161728 | bytes 16793600 | tf_op jit(solution)/shard_map/reduce_sum | solution.py:19
  267.7 0.0 copy-start
  267.7 29.3 %fusion = f32[4096,2048]{1,0:T(8,128)} fusion(bf16[1024,2048]{1,0:T(8,128)(2,1)} %all-gather.8.cloned.1.call-done, bf16[1024,4096]{1,0:T(8,128)(2,1)} %all-gather.6.cloned.1.call-done, bf16[1024,4096]{1,0:T(8,128)(2,1)} %all-gather.4.cloned.1.call-done), kind=kOutput, calls=%fused_computation.5 | convolution fusion | flops 17196646400 | bytes 54525952 | tf_op jit(solution)/shard_map/dot_general | solution.py:16
  297.0 24.5 %reduce-scatter.3.cloned.1.call-done = bf16[128,4096]{1,0:T(8,128)(2,1)} async-done(((bf16[1024,4096]{1,0:T(8,128)(2,1)}), bf16[128,4096]{1,0:T(8,128)(2,1)}) %reduce-scatter.3.cloned.1.call-update) | async-done | bytes 1048592 | tf_op jit(solution)/shard_map/reduce_scatter | solution.py:21
  321.5 0.0 copy-done
  321.5 2.5 multiply_convert_fusion.1
  324.0 51.9 %reduce-scatter.5.cloned.1.call-done = bf16[256,2048]{1,0:T(8,128)(2,1)} async-done(((bf16[1024,2048]{1,0:T(8,128)(2,1)}), bf16[256,2048]{1,0:T(8,128)(2,1)}) %reduce-scatter.5.cloned.1.call-update) | async-done | bytes 1048592 | tf_op jit(solution)/shard_map/reduce_scatter | solution.py:32
  (1 shorter events, 0.0 us)
Async XLA Ops:
  7.2 58.1 %all-gather.8.cloned.1.call-start = ((), (), s32[]{:S(2)}) async-start(), calls=%async_computation.4 | async-start | bytes 5242880 | tf_op jit(solution)/shard_map/all_gather | solution.py:8
  7.9 141.1 %all-gather.6.cloned.1.call-start = ((), (), s32[]{:S(2)}) async-start(), calls=%async_computation.3 | async-start | bytes 9437184 | tf_op jit(solution)/shard_map/all_gather | solution.py:11
  8.6 222.6 %all-gather.4.cloned.1.call-start = ((), (), s32[]{:S(2)}) async-start(), calls=%async_computation.2 | async-start | bytes 9437184 | tf_op jit(solution)/shard_map/all_gather | solution.py:10
  9.4 312.1 %reduce-scatter.3.cloned.1.call-start = ((), (), s32[]{:S(2)}) async-start(), calls=%async_computation.5 | async-start | bytes 9437184 | tf_op jit(solution)/shard_map/reduce_scatter | solution.py:21
  88.3 169.3 %copy-start.1 = (bf16[4096]{0:T(1024)(128)(2,1)S(1)}, bf16[4096]{0:T(1024)(128)(2,1)}, u32[]{:S(2)}) copy-start(bf16[4096]{0:T(1024)(128)(2,1)} %param.9) | copy-start | bytes 24580
  88.3 287.6 %reduce-scatter.5.cloned.1.call-start = ((), (), s32[]{:S(2)}) async-start(), calls=%async_computation.6 | async-start | bytes 5242880 | tf_op jit(solution)/shard_map/reduce_scatter | solution.py:32
  267.7 53.9 %copy-start = (bf16[128,4096]{1,0:T(8,128)(2,1)S(1)}, bf16[128,4096]{1,0:T(8,128)(2,1)}, u32[]{:S(2)}) copy-start(bf16[128,4096]{1,0:T(8,128)(2,1)} %param.7) | copy-start | bytes 3145732
Sparse Core Ops, SparseCore 0:
  9.8 55.3 all-gather.7
  66.9 82.0 all-gather.5
  150.6 80.5 all-gather.3
  233.3 88.1 reduce-scatter.2
  324.9 51.0 reduce-scatter.4
where the time goes:
time: 383 us
  waiting for transfers between devices  277 us (72%)
  matrix products  78.8 us (21%)
  between operations  13.8 us (4%)
  other arithmetic  12.5 us (3%)
    all_gather x1, waiting for transfers between devices, on_device(): lax.all_gather(out_grad, 'col', axis=0, tiled=True)  82.2 us
    all_gather x1, waiting for transfers between devices, on_device(): lax.all_gather(base_input, 'col', axis=0, tiled=True)  60.6 us
    all_gather x1, waiting for transfers between devices, on_device(): input_panel = lax.all_gather(layer_input, 'row', axis=0, tiled=True)  55.9 us
    reduce_scatter x1, waiting for transfers between devices, on_device(): lax.psum_scatter(jnp.dot(rows, cross_weight, preferred_element_type=jnp.f...  51.9 us
    dot_general x1, matrix products, on_device(): lax.dot_general(hidden_panel, input_panel, (((0,), (0,)), ((), ())), pref...  29.3 us
    dot_general x1, matrix products, on_device(): jnp.dot(rows, cross_weight, preferred_element_type=jnp.float32)  26.4 us
    reduce_scatter x1, waiting for transfers between devices, on_device(): lax.psum_scatter(lax.dot_general(rows, cross_weight, (((1,), (1,)), ((),...  24.5 us
    dot_general x1, matrix products, on_device(): lax.dot_general(rows, cross_weight, (((1,), (1,)), ((), ())), preferred_e...  23 us
  transfers between devices with their start and end apart: 5, of which 5 were waited for; matrix products, arithmetic and copies ran while one was open for 24% of the time, Pallas kernels for 0%

commit v1 on v0

v1 whole, which is shorter than its diff:
```python
import functools

import jax
import jax.numpy as jnp
from jax import lax
from jax.experimental import pallas as pl
from jax.experimental.pallas import tpu as pltpu
from jax.sharding import PartitionSpec as P

F32, BF16 = jnp.float32, jnp.bfloat16
ANY = pl.BlockSpec(memory_space=pl.ANY)
SMEM = pl.BlockSpec(memory_space=pltpu.SMEM)
VMEM = pl.BlockSpec(memory_space=pltpu.VMEM)
DMA = pltpu.SemaphoreType.DMA
MIB = 1024 * 1024

CORE, Z, ROW, FIRST, REL = range(5)
PIECES = 2


def params(mib):
    return pltpu.CompilerParams(vmem_limit_bytes=mib * MIB)


def in_hbm(*arrays):
    return [pltpu.with_memory_space_constraint(a, pltpu.HBM) for a in arrays]


def cost(flops, nbytes):
    return pl.CostEstimate(flops=1, bytes_accessed=1, transcendentals=0)


def turned(place, apart):
    other = jnp.where(apart == 1, 2, jnp.where(apart == 2, 1, apart))
    return jnp.where(place[CORE] == 0, apart, other)


def x_sources(place, block, half, own, got):
    lanes = own.shape[0] // 2
    apart = turned(place, block ^ place[ROW])
    last = place[REL] == 3
    conds = [apart == 0, apart == 1]
    conds.append(jnp.where(last, apart == 3, apart == 2))
    conds.append(jnp.where(last, apart == 2, apart == 3))
    refs = (own,) + tuple(got)
    return [(ref.at[pl.ds(half * lanes, lanes)], cond) for ref, cond in zip(refs, conds) if ref is not None]


def load_x(place, block, own, got, held, at, sem):
    for half in range(2):
        slot = at + jnp.where(place[CORE] == half, 0, 1)
        for ref, cond in x_sources(place, block, half, own, got):

            @pl.when(cond)
            def _():
                pltpu.make_async_copy(ref, held.at[slot], sem.at[slot]).start()


def wait_x(own, held, at, sem):
    lanes = own.shape[0] // 2
    for k in (at, at + 1):
        pltpu.make_async_copy(own.at[pl.ds(0, lanes)], held.at[k], sem.at[k]).wait()


def pre_block(place, index):
    middle = jnp.logical_or(place[Z] == 1, place[Z] == 2)
    rel = {0: 0, 1: 1, 2: jnp.where(middle, 3, 2), 3: jnp.where(middle, 2, 3)}[index]
    return rel ^ place[FIRST]


def back_block(place, slot):
    low = place[Z] < 2
    return (place[Z], place[Z] ^ 1, jnp.where(low, 2, 1), jnp.where(low, 3, 0))[slot]


def pre_kernel(indices, n_got, chunks, place, own, *refs):
    got = list(refs[:n_got]) + [None] * (3 - n_got)
    w, refs = refs[n_got], refs[n_got + 1 :]
    n_out = 2 * len(indices)
    n_ref = (1 + PIECES) * len(indices)
    outs, (held, held_w, held_y, sem, sem_w, sem_y) = refs[:n_ref], refs[n_ref:]
    lanes = held.shape[1]
    tile = w.shape[0] // chunks

    def w_copy(i):
        part = pl.ds(pl.multiple_of(i * tile, tile), tile)
        return pltpu.make_async_copy(w.at[part], held_w.at[part], sem_w.at[i])

    def y_copy(i, k, out, at):
        part = pl.ds(pl.multiple_of(at * tile, tile), tile)
        return pltpu.make_async_copy(held_y.at[i, pl.ds(k * lanes, lanes)], out.at[:, part], sem_y.at[i, k])

    def start_y(i):
        run = chunks // PIECES
        for b in range(len(indices)):
            mine, *other = outs[(1 + PIECES) * b : (1 + PIECES) * (b + 1)]
            y_copy(i, 2 * b, mine, i).start()
            for piece, out in enumerate(other):

                @pl.when(i // run == piece)
                def _():
                    y_copy(i, 2 * b + 1, out, i % run).start()

    for i, index in enumerate(indices):
        load_x(place, pre_block(place, index), own, got, held, 2 * i, sem)

    def start(i, _):
        w_copy(i).start()
        return _

    lax.fori_loop(0, chunks, start, 0)
    for i in range(len(indices)):
        wait_x(own, held, 2 * i, sem)

    def step(i, _):
        w_copy(i).wait()
        x = held[...].reshape(n_out * lanes, held.shape[2])
        rows = held_w[pl.ds(pl.multiple_of(i * tile, tile), tile)]
        held_y[i] = lax.dot_general(x, rows, (((1,), (1,)), ((), ())), preferred_element_type=F32).astype(BF16)
        start_y(i)
        return _

    lax.fori_loop(0, chunks, step, 0)

    def finish(i, _):
        for k in range(n_out):
            y_copy(i, k, outs[0], 0).wait()
        return _

    lax.fori_loop(0, chunks, finish, 0)


def pre_parts(place, own, got, w, indices, chunks):
    rows, depth = own.shape
    lanes, wide, outs = rows // 2, w.shape[0], 2 * len(indices)
    return pl.pallas_call(
        functools.partial(pre_kernel, tuple(indices), len(got), chunks),
        in_specs=[SMEM] + [ANY] * (2 + len(got)),
        out_specs=[ANY] * ((1 + PIECES) * len(indices)),
        scratch_shapes=[
            pltpu.VMEM((outs, lanes, depth), BF16),
            pltpu.VMEM((wide, depth), BF16),
            pltpu.VMEM((chunks, outs * lanes, wide // chunks), BF16),
            DMA((outs,)),
            DMA((chunks,)),
            DMA((chunks, outs)),
        ],
        out_shape=[jax.ShapeDtypeStruct((lanes, n), BF16) for n in [wide] + [wide // PIECES] * PIECES]
        * len(indices),
        compiler_params=params(28),
        cost_estimate=cost(2 * outs * lanes * depth * wide, 2 * wide * depth),
        name="pre_parts",
    )(place, *in_hbm(own, *got, w))


def back_kernel(slots, by_role, n_prior, chunks, place, *refs):
    n_h = 2 * len(slots)
    hs, w, refs = refs[:n_h], refs[n_h], refs[n_h + 1 + n_prior :]
    outs, (held, held_w, held_y, sem, sem_w, sem_y) = refs[:-6], refs[-6:]
    lanes = held.shape[1]
    tile = w.shape[1] // chunks

    def w_copy(i):
        part = pl.ds(pl.multiple_of(i * tile, tile), tile)
        return pltpu.make_async_copy(w.at[:, part], held_w.at[i], sem_w.at[i])

    def h_copy(k):
        slot = k // 2 * 2 + (place[CORE] if k % 2 == 0 else 1 - place[CORE])
        return pltpu.make_async_copy(hs[k], held.at[slot], sem.at[k])

    def y_copy(i, k, out):
        part = pl.ds(pl.multiple_of(i * tile, tile), tile)
        return pltpu.make_async_copy(held_y.at[i, pl.ds(2 * k * lanes, 2 * lanes)], out.at[:, part], sem_y.at[i, k])

    def start_y(i, k):
        if not by_role:
            y_copy(i, k, outs[k]).start()
            return
        role = turned(place, back_block(place, slots[k]) ^ place[ROW])
        for at, out in enumerate(outs):

            @pl.when(role == at)
            def _():
                y_copy(i, k, out).start()

    for k in range(n_h):
        h_copy(k).start()

    def start(i, _):
        w_copy(i).start()
        return _

    lax.fori_loop(0, chunks, start, 0)
    for k in range(n_h):
        h_copy(k).wait()

    def step(i, _):
        w_copy(i).wait()
        h = held[...].reshape(n_h * lanes, held.shape[2])
        held_y[i] = jnp.dot(h, held_w[i], preferred_element_type=F32).astype(BF16)
        for k in range(len(slots)):
            start_y(i, k)
        return _

    lax.fori_loop(0, chunks, step, 0)

    def finish(i, _):
        for k in range(len(slots)):
            y_copy(i, k, outs[0]).wait()
        return _

    lax.fori_loop(0, chunks, finish, 0)


def back_parts(place, slots, hs, w, chunks, prior=None, by_role=True):
    lanes, depth = hs[0].shape
    wide, n_h = w.shape[1], len(hs)
    block = pltpu.HBM((2 * lanes, wide), BF16)
    prior = list(prior or [])
    return pl.pallas_call(
        functools.partial(back_kernel, tuple(slots), by_role, len(prior), chunks),
        in_specs=[SMEM] + [ANY] * (n_h + 1 + len(prior)),
        out_specs=[ANY] * (4 if by_role else len(slots)),
        scratch_shapes=[
            pltpu.VMEM((n_h, lanes, depth), BF16),
            pltpu.VMEM((chunks, depth, wide // chunks), BF16),
            pltpu.VMEM((chunks, n_h * lanes, wide // chunks), BF16),
            DMA((n_h,)),
            DMA((chunks,)),
            DMA((chunks, len(slots))),
        ],
        out_shape=[block] * (4 if by_role else len(slots)),
        input_output_aliases={n_h + 2 + k: k for k in range(len(prior))},
        compiler_params=params(28),
        cost_estimate=cost(2 * n_h * lanes * depth * wide, 2 * wide * depth),
        name="back_parts",
    )(place, *in_hbm(*hs, w, *prior))


def weight_kernel(n_h, n_prior, place, own, *refs):
    got, hs, (grad, bias, held, sem) = refs[:3], refs[3 : 3 + n_h], refs[3 + n_h + n_prior :]

    @pl.when(pl.program_id(0) == 0)
    def _():
        for slot in range(n_h // 2):
            load_x(place, back_block(place, slot), own, got, held, 2 * slot, sem)
        for slot in range(n_h // 2):
            wait_x(own, held, 2 * slot, sem)

    lanes = held.shape[1]
    h = jnp.concatenate([ref[...] for ref in hs], axis=0)
    x = held[...].reshape(n_h * lanes, held.shape[2])
    grad[...] = lax.dot_general(h, x, (((0,), (0,)), ((), ())), preferred_element_type=F32)
    bias[...] = jnp.sum(h.astype(F32), axis=0, keepdims=True)


def weight_grads(place, own, got, hs, tile, first, count, prior=()):
    lanes, feats = hs[0].shape
    wide, n_h = own.shape[1], len(hs)
    return pl.pallas_call(
        functools.partial(weight_kernel, n_h, len(prior)),
        grid=(count,),
        in_specs=[SMEM]
        + [ANY] * 4
        + [pl.BlockSpec((lanes, tile), lambda i: (0, first + i))] * n_h
        + [ANY] * len(prior),
        out_specs=[pl.BlockSpec((tile, wide), lambda i: (first + i, 0)), pl.BlockSpec((1, tile), lambda i: (0, i))],
        scratch_shapes=[pltpu.VMEM((n_h, lanes, wide), BF16), DMA((n_h,))],
        out_shape=[pltpu.HBM((feats, wide), F32), jax.ShapeDtypeStruct((1, count * tile), F32)],
        input_output_aliases={5 + n_h + k: k for k in range(len(prior))},
        compiler_params=params(26),
        cost_estimate=cost(2 * n_h * lanes * wide * feats, 4 * wide * feats),
        name="weight_grads",
    )(place, *in_hbm(own, *got), *in_hbm(*hs), *in_hbm(*prior))


def wide_sum(*parts):
    parts = [jnp.concatenate(p, axis=1) if isinstance(p, list) else p for p in parts]
    return functools.reduce(lambda a, b: a + b, [p.astype(F32) for p in parts])


def add_kernel(*refs):
    q, others, out = refs[0], refs[1:-1], refs[-1]
    pieces, wide = others[-PIECES:], others[:-PIECES]
    run = pieces[0].shape[1]
    for k, piece in enumerate(pieces):
        part = pl.ds(k * run, run)
        total = q[:, part].astype(F32) + piece[...].astype(F32)
        for ref in wide:
            total += ref[:, part].astype(F32)
        out[:, part] = total.astype(out.dtype)


def add_parts(q, pieces, *more):
    return pl.pallas_call(
        add_kernel,
        in_specs=[VMEM] * (1 + len(more) + len(pieces)),
        out_specs=VMEM,
        out_shape=jax.ShapeDtypeStruct(q.shape, BF16),
        compiler_params=params(12),
        cost_estimate=cost(0, 0),
        name="add_parts",
    )(q, *more, *pieces)


def line_pairs(hops):
    return [(2 * a + core, 2 * b + core) for a, b in hops for core in (0, 1)]


def after(value, *done):
    return lax.optimization_barrier((value,) + done)[0]


def on_line(base_input, layer_input, out_grad, cross_weight, cross_bias):
    lanes = base_input.shape[0]
    col, row = lax.axis_index("col"), lax.axis_index("row")
    z, core = col // 2, col % 2
    end = jnp.logical_or(z == 0, z == 3)
    first = jnp.where(z < 2, 3, 0)
    place = jnp.stack([core, z, row, first, row ^ first]).astype(jnp.int32)

    def across(a, name):
        with jax.named_scope(name):
            return jax.tree.map(lambda one: lax.ppermute(one, "col", [(i, i ^ 1) for i in range(8)]), a)

    def line(a, hops, name):
        with jax.named_scope(name):
            return lax.ppermute(a, "col", line_pairs(hops))

    def plane(a, hops, name):
        pairs = [(8 * f + 2 * k + c, 8 * t + 2 * k + c) for k in range(4) for c, f, t in hops(k)]
        with jax.named_scope(name):
            return lax.ppermute(a, ("row", "col"), pairs)

    def first_way(k):
        return [(c, r, r ^ (1 + c)) for c in (0, 1) for r in range(4)]

    def second_way(k):
        return [(c, r, r ^ (2 - c)) for c in (0, 1) for r in range(4)]

    outer, inner = [(0, 1), (1, 0), (2, 3), (3, 2)], [(1, 2), (2, 1)]
    outwards, inwards = [(1, 0), (2, 3)], [(0, 1), (3, 2)]

    cross_weight = pltpu.with_memory_space_constraint(cross_weight, pltpu.VMEM)
    def pre(indices, got, *done):
        out = pre_parts(after(place, *done), layer_input, got, cross_weight, indices, 8)
        each = 1 + PIECES
        return [part for k in range(len(indices)) for part in (out[each * k], out[each * k + 1 : each * (k + 1)])]

    def back(slots, hs, *done, prior=None, by_role=True):
        return back_parts(after(place, *done), slots, hs, cross_weight, 8, prior, by_role)

    def both(*values, done):
        return lax.optimization_barrier(values + tuple(done))[: len(values)]

    relays = turned(place, place[REL]) == 1
    p1 = plane(layer_input, first_way, "p1")
    own_h = (out_grad.astype(F32) * base_input.astype(F32)).astype(BF16)
    a0, b0 = line(own_h, outer, "a0"), line(own_h, inner, "b0")
    h0 = across(own_h, "h0")
    to_p2 = jnp.where(relays, p1, layer_input)
    to_p3 = jnp.where(relays, layer_input, p1)
    p2 = plane(to_p2, second_way, "p2")
    roles = back((0,), (own_h, h0), to_p2, to_p3)

    a0, b0, p2, to_p3 = both(a0, b0, p2, to_p3, done=roles)
    a1, b1 = line(b0, outwards, "a1"), line(a0, inner, "b1")
    p3 = plane(to_p3, second_way, "p3")
    h1 = across(a0, "h1")
    q0, o0 = pre((0,), (p1, p2))
    o0 = across(o0, "o0")
    to_ra1 = add_parts(after(q0, p3), o0)
    ra1 = line(to_ra1, inwards, "ra1")
    q1, o1, q2, o2 = pre((1, 2), (p1, p2, p3), to_ra1)
    o1, o2 = across(o1, "o1"), across(o2, "o2")

    a1, b1 = both(a1, b1, done=(q1,))
    a2 = line(b1, outwards, "a2")
    s2 = jnp.where(end, a1, b0)
    h2 = across(s2, "h2")

    ra1, q0 = both(ra1, q0, done=(s2,))
    to_rb2, to_ra2 = add_parts(q0, o0, ra1), add_parts(q1, o1)
    rb2, ra2 = line(to_rb2, inner, "rb2"), line(to_ra2, inwards, "ra2")
    roles = back((1, 2), (a0, h1, s2, h2), to_rb2, to_ra2, *o2, prior=roles)

    a2, *roles = both(a2, *roles, done=())
    s3 = jnp.where(end, a2, b1)
    h3 = across(s3, "h3")
    e1, f1 = plane(roles[1], first_way, "e1"), plane(roles[3], first_way, "f1")
    rb2, ra2 = both(rb2, ra2, done=(s3,))
    (part,) = back((3,), (s3, h3), roles[0], rb2, ra2, by_role=False)

    rb2, ra2 = both(rb2, ra2, done=(part,))
    to_ra3, to_rb3 = add_parts(q2, o2, rb2), add_parts(q1, o1, ra2)
    ra3, rb3 = line(to_ra3, outer, "ra3"), line(to_rb3, inner, "rb3")

    mine, relayed = roles[0], roles[2]
    last_of = [3, 3, 0, 0]

    def last_first(k):
        return [(0, f ^ last_of[k], t ^ last_of[k]) for f, t in ((3, 2), (1, 0))] + [
            (1, f ^ last_of[k], t ^ last_of[k]) for f, t in ((3, 1), (2, 0))
        ]

    def last_second(k):
        return [(0, 2 ^ last_of[k], last_of[k]), (1, 1 ^ last_of[k], last_of[k])]

    l1 = plane(part, last_first, "l1")
    f1, e1 = both(f1, e1, done=(part,))
    to_e2 = wide_sum(relayed, f1).astype(BF16)
    e2 = plane(to_e2, second_way, "e2")
    q3, o3 = pre((3,), (p1, p2, p3), to_e2, to_ra3, to_rb3)
    o3 = across(o3, "o3")
    to_l2 = wide_sum(part, after(l1, q3)).astype(BF16)
    l2 = plane(to_l2, last_second, "l2")
    hs = (own_h, h0, a0, h1, s2, h2, s3, h3)
    grad, bias = weight_grads(after(place, to_l2), layer_input, (p1, p2, p3), hs, 512, 0, base_input.shape[1] // 512)
    ra3, rb3, *o3 = both(ra3, rb3, *o3, done=(bias,))
    preact = wide_sum(ra3, rb3, q3, o3) + cross_bias.astype(F32)[None, :]
    base_grad = (out_grad.astype(F32) * preact).astype(BF16)
    l2, e2 = both(l2, e2, done=(base_grad,))
    branch = jnp.where(row == back_block(place, 3), wide_sum(to_l2, l2), wide_sum(mine, e1, e2)).astype(BF16)
    return (grad, bias[0], base_grad, branch)


def on_any(base_input, layer_input, out_grad, cross_weight, cross_bias):
    input_panel = lax.all_gather(layer_input, "row", axis=0, tiled=True)
    hidden = (out_grad.astype(F32) * base_input.astype(F32)).astype(BF16)
    hidden_panel = lax.all_gather(hidden, "col", axis=0, tiled=True)
    weight_grad = lax.dot_general(
        hidden_panel, input_panel, (((0,), (0,)), ((), ())), preferred_element_type=F32
    )
    bias_grad = jnp.sum(hidden_panel, axis=0, dtype=F32)
    part = lax.dot_general(input_panel, cross_weight, (((1,), (1,)), ((), ())), preferred_element_type=F32)
    preact = lax.psum_scatter(part.astype(BF16), "col", scatter_dimension=0, tiled=True).astype(F32)
    preact = preact + cross_bias.astype(F32)[None, :]
    base_grad = (out_grad.astype(F32) * preact).astype(BF16)
    part = jnp.dot(hidden_panel, cross_weight, preferred_element_type=F32).astype(BF16)
    branch = lax.psum_scatter(part, "row", scatter_dimension=0, tiled=True)
    return (weight_grad, bias_grad, base_grad, branch)


def solution(mesh):
    in_specs = (P("col", "row"), P("row", "col"), P("col", "row"), P("row", "col"), P("row"))
    out_specs = (P("row", "col"), P("row"), P("col", "row"), P("row", "col"))
    body = on_line if (mesh.shape["row"], mesh.shape["col"]) == (4, 8) else on_any
    return jax.shard_map(body, mesh=mesh, in_specs=in_specs, out_specs=out_specs, check_vma=False)
```

time: 383 us -> 188 us (0.49)
  waiting for transfers between devices: 277 us -> 27.5 us
  Pallas kernels: 0 us -> 93.5 us
  matrix products: 78.8 us -> 0 us
  starting transfers between devices: 0.19 us -> 44.2 us
  between operations: 13.8 us -> 1.07 us
  local copies, waits for them, and re-layouts: 0.01 us -> 5.07 us
    all_gather x3 -> x0, waiting for transfers between devices: 199 us -> none  [the longest x1 82.2 us: on_device(): lax.all_gather(out_grad, 'col', axis=0, tiled=True)]
    pallas_call x0 -> x12, Pallas kernels: none -> 93.5 us  [the longest x3 33.6 us: back_parts(): pl.pallas_call(functools.partial(back_kernel, tuple(slots), by_role, len(...]
    dot_general x3 -> x0, matrix products: 78.8 us -> none  [the longest x1 29.3 us: on_device(): lax.dot_general(hidden_panel, input_panel, (((0,), (0,)), ((), ())), pref...]
    reduce_scatter x2 -> x0, waiting for transfers between devices: 76.4 us -> none  [the longest x1 51.9 us: on_device(): lax.psum_scatter(jnp.dot(rows, cross_weight, preferred_element_type=jnp.f...]
    ppermute x0 -> x30, starting transfers between devices: none -> 44.2 us  [the longest x10 26.8 us: line(): return lax.ppermute(a, 'col', line_pairs(hops))]
    ppermute x0 -> x30, waiting for transfers between devices: none -> 27.5 us  [the longest x8 17.7 us: plane(): return lax.ppermute(a, ('row', 'col'), pairs)]
    reduce_sum x1 -> x0, other arithmetic: 10 us -> none  [on_device(): bias_grad = jnp.sum(hidden_panel, axis=0, dtype=jnp.float32)]
    convert_element_type x2 -> x6, other arithmetic: 2.51 us -> 12 us  [the longest x1 3.77 us: on_line(): base_grad = (out_grad.astype(F32) * preact).astype(BF16)]
  transfers between devices with their start and end apart: 5 -> 30, of which waited for: 5 -> 9; matrix products, arithmetic and copies ran while one was open for 24% -> 6% of each run, Pallas kernels for 0% -> 50%
where the time goes in v1:
time: 188 us; the launch traced here: 186 us
  Pallas kernels  93.5 us (50%)
  starting transfers between devices  44.2 us (24%)
  waiting for transfers between devices  27.5 us (15%)
  other arithmetic  15 us (8%)
  local copies, waits for them, and re-layouts  5.07 us (3%)
    pallas_call x3, Pallas kernels, back_parts(): pl.pallas_call(functools.partial(back_kernel, tuple(slots), by_role, len(...  33.6 us
    pallas_call x3, Pallas kernels, pre_parts(): pl.pallas_call(functools.partial(pre_kernel, tuple(indices), len(got), ch...  33.1 us
    ppermute x10, starting transfers between devices, line(): return lax.ppermute(a, 'col', line_pairs(hops))  26.8 us
    pallas_call x1, Pallas kernels, weight_grads(): pl.pallas_call(functools.partial(weight_kernel, n_h, len(prior)), grid=(c...  25.2 us
    ppermute x8, waiting for transfers between devices, plane(): return lax.ppermute(a, ('row', 'col'), pairs)  17.7 us
    ppermute x8, starting transfers between devices, plane(): return lax.ppermute(a, ('row', 'col'), pairs)  14.7 us
    ppermute x10, waiting for transfers between devices, line(): return lax.ppermute(a, 'col', line_pairs(hops))  7.94 us
    unnamed x40, local copies, waits for them, and re-layouts  4.99 us
  transfers between devices with their start and end apart: 30, of which 9 were waited for; matrix products, arithmetic and copies ran while one was open for 6% of the time, Pallas kernels for 50%

profile of v1, /device:TPU:0, one launch (start us, length us, event | category | flops | bytes accessed | tf_op | source)
XLA Modules:
  0.0 186.4 jit_solution(8478694473731989898)
XLA Ops:
  0.6 3.0 %collective-permute-start.2 = (bf16[256,2048]{1,0:T(8,128)(2,1)}, bf16[256,2048]{1,0:T(8,128)(2,1)S(1)}, u32[]{:S(2)}, u32[]{:S(2)}) collective-permute-start(bf16[256,2048]{1,0:T(8,128)(2,1)} %own.7), channel_id=1, source_target_pairs={{0,8},{8,0},{16,24},{24,16},{1,17},{9,25},{17,1},{25,9},{2,10},{10... | collective-permute-start | bytes 3145736 | tf_op jit(solution)/shard_map/p1/ppermute | solution.py:333
  3.6 1.8 fusion.refs_0_.refs_3_
  5.4 0.1 collective-permute-start.4
  5.5 1.6 collective-permute-start
  7.2 1.6 collective-permute-start.1
  8.8 7.8 %collective-permute-done.2.refs_0_ = bf16[256,2048]{1,0:T(8,128)(2,1)S(1)} collective-permute-done((bf16[256,2048]{1,0:T(8,128)(2,1)}, bf16[256,2048]{1,0:T(8,128)(2,1)S(1)}, u32[]{:S(2)}, u32[]{:S(2)}) %collective-permute-start.2) | collective-permute-done | bytes 1048608 | tf_op jit(solution)/shard_map/p1/ppermute | solution.py:333
  16.6 1.5 broadcast_select_fusion.2
  18.2 0.1 copy-done.1
  18.3 2.0 %collective-permute-start.3 = (bf16[256,2048]{1,0:T(8,128)(2,1)}, bf16[256,2048]{1,0:T(8,128)(2,1)S(1)}, u32[]{:S(2)}, u32[]{:S(2)}) collective-permute-start(bf16[256,2048]{1,0:T(8,128)(2,1)} %get-tuple-element.115), channel_id=1, source_target_pairs={{0,16},{8,24},{16,0},{24,8},{1,9},{9,1},{17,25},{25,17},{2,18},{10... | collective-permute-start | bytes 3145736 | tf_op jit(solution)/shard_map/p2/ppermute | solution.py:333
  20.3 0.1 stack.23.place
  20.4 9.6 %back_parts.3 = (bf16[256,2048]{1,0:T(8,128)(2,1)}, bf16[256,2048]{1,0:T(8,128)(2,1)}, bf16[256,2048]{1,0:T(8,128)(2,1)}, bf16[256,2048]{1,0:T(8,128)(2,1)}) custom-call(s32[5]{0:T(128)S(1)} %stack.23.place, bf16[128,4096]{1,0:T(8,128)(2,1)} %copy-done.5, bf16[128,4096]{1,0:T(8,128)(2,1)} %collective-permute-done.4.refs_1_.refs_4_, bf16[4096,2048]{1,0:T(8,128)(2,1)} %refs_3_.3), custom_call_target="tpu_custom_call" | custom-call | flops 1 | bytes 1 | tf_op jit(solution)/shard_map/back_parts/pallas_call | solution.py:220
  30.0 1.2 collective-permute-done.refs_0_.refs_5_
  31.2 2.1 %collective-permute-done.3.refs_1_ = bf16[256,2048]{1,0:T(8,128)(2,1)S(1)} collective-permute-done((bf16[256,2048]{1,0:T(8,128)(2,1)}, bf16[256,2048]{1,0:T(8,128)(2,1)S(1)}, u32[]{:S(2)}, u32[]{:S(2)}) %collective-permute-start.3) | collective-permute-done | bytes 1048608 | tf_op jit(solution)/shard_map/p2/ppermute | solution.py:333
  33.3 2.0 %collective-permute-start.7 = (bf16[256,2048]{1,0:T(8,128)(2,1)}, bf16[256,2048]{1,0:T(8,128)(2,1)}, u32[]{:S(2)}, u32[]{:S(2)}) collective-permute-start(bf16[256,2048]{1,0:T(8,128)(2,1)} %get-tuple-element.68), channel_id=1, source_target_pairs={{0,16},{8,24},{16,0},{24,8},{1,9},{9,1},{17,25},{25,17},{2,18},{10... | collective-permute-start | bytes 3145736 | tf_op jit(solution)/shard_map/p3/ppermute | solution.py:333
  35.4 1.3 collective-permute-start.5
  36.6 1.7 collective-permute-start.6
  38.4 9.2 %pre_parts.3 = (bf16[128,4096]{1,0:T(8,128)(2,1)S(1)}, bf16[128,2048]{1,0:T(8,128)(2,1)S(1)}, bf16[128,2048]{1,0:T(8,128)(2,1)S(1)}) custom-call(s32[5]{0:T(128)S(1)} %stack.23.place, bf16[256,2048]{1,0:T(8,128)(2,1)} %own.7, bf16[256,2048]{1,0:T(8,128)(2,1)} %copy-done.1, bf16[256,2048]{1,0:T(8,128)(2,1)} %copy-done.2, bf16[4096,2048]{1,0:T(8,128)(2,1)} %refs_3_.3), custom_call_target="tpu_custom_call" | custom-call | flops 1 | bytes 1 | tf_op jit(solution)/shard_map/pre_parts/pallas_call | solution.py:136
  47.5 0.1 collective-permute-start.8
  47.6 0.5 collective-permute-start.9
  48.1 0.3 collective-permute-done.7.refs_2_
  48.5 1.0 collective-permute-done.8.refs_1_.refs_2_
  49.5 0.7 collective-permute-done.9.refs_2_.refs_3_
  50.3 0.2 add_parts.5
  50.5 9.3 %collective-permute-start.11 = (bf16[128,4096]{1,0:T(8,128)(2,1)S(1)}, bf16[128,4096]{1,0:T(8,128)(2,1)S(1)}, u32[]{:S(2)}, u32[]{:S(2)}) collective-permute-start(bf16[128,4096]{1,0:T(8,128)(2,1)S(1)} %add_parts.5), channel_id=1, source_target_pairs={{0,2},{1,3},{6,4},{7,5},{8,10},{9,11},{14,12},{15,13},{16,18},{17,... | collective-permute-start | bytes 3145736 | tf_op jit(solution)/shard_map/ra1/ppermute | solution.py:328
  59.8 14.2 %pre_parts.4 = (bf16[128,4096]{1,0:T(8,128)(2,1)S(1)}, bf16[128,2048]{1,0:T(8,128)(2,1)S(1)}, bf16[128,2048]{1,0:T(8,128)(2,1)S(1)}, bf16[128,4096]{1,0:T(8,128)...) custom-call(s32[5]{0:T(128)S(1)} %stack.23.place, bf16[256,2048]{1,0:T(8,128)(2,1)} %own.7, ...), custom_call_target="tpu_custom_call" | custom-call | flops 1 | bytes 1 | tf_op jit(solution)/shard_map/pre_parts/pallas_call | solution.py:136
  74.0 0.1 collective-permute-start.12
  74.1 0.5 collective-permute-start.13
  74.6 1.3 broadcast_select_fusion.1.refs_2_.refs_7_
  75.9 0.2 collective-permute-start.17
  76.1 1.3 collective-permute-start.10
  77.4 0.5 collective-permute-start.14
  77.9 4.5 %collective-permute-done.11.refs_1_ = bf16[128,4096]{1,0:T(8,128)(2,1)S(1)} collective-permute-done((bf16[128,4096]{1,0:T(8,128)(2,1)S(1)}, bf16[128,4096]{1,0:T(8,128)(2,1)S(1)}, u32[]{:S(2)}, u32[]{:S(2)}) %collective-permute-start.11) | collective-permute-done | bytes 1048608 | tf_op jit(solution)/shard_map/ra1/ppermute | solution.py:328
  82.4 0.2 add_parts.7
  82.6 0.4 add_parts.6
  83.0 4.5 %collective-permute-start.19 = (bf16[128,4096]{1,0:T(8,128)(2,1)S(1)}, bf16[128,4096]{1,0:T(8,128)(2,1)S(1)}, u32[]{:S(2)}, u32[]{:S(2)}) collective-permute-start(bf16[128,4096]{1,0:T(8,128)(2,1)S(1)} %add_parts.7), channel_id=1, source_target_pairs={{0,2},{1,3},{6,4},{7,5},{8,10},{9,11},{14,12},{15,13},{16,18},{17,... | collective-permute-start | bytes 3145736 | tf_op jit(solution)/shard_map/ra2/ppermute | solution.py:328
  87.5 0.7 collective-permute-start.18
  88.3 0.9 copy-done.6
  89.2 1.0 copy-done.7
  90.2 14.5 %back_parts.4 = (bf16[256,2048]{1,0:T(8,128)(2,1)}, bf16[256,2048]{1,0:T(8,128)(2,1)}, bf16[256,2048]{1,0:T(8,128)(2,1)}, bf16[256,2048]{1,0:T(8,128)(2,1)}) custom-call(s32[5]{0:T(128)S(1)} %stack.23.place, bf16[128,4096]{1,0:T(8,128)(2,1)} %collective-permute-done.refs_0_.refs_5_, ...), custom_call_target="tpu_custom_call", output_to_operand_aliasing={{0}: (6, {}), {1}: (7, {}), {2}: (8, {}), {3}: (9, {})} | custom-call | flops 1 | bytes 1 | tf_op jit(solution)/shard_map/back_parts/pallas_call | solution.py:220
  104.8 0.1 broadcast_select_fusion.refs_0_.refs_9_
  104.9 0.3 collective-permute-start.20
  105.2 1.1 copy-done.14
  106.3 1.5 collective-permute-start.22
  107.8 0.5 collective-permute-start.23
  108.3 2.2 %collective-permute-done.19.refs_1_ = bf16[128,4096]{1,0:T(8,128)(2,1)S(1)} collective-permute-done((bf16[128,4096]{1,0:T(8,128)(2,1)S(1)}, bf16[128,4096]{1,0:T(8,128)(2,1)S(1)}, u32[]{:S(2)}, u32[]{:S(2)}) %collective-permute-start.19) | collective-permute-done | bytes 1048608 | tf_op jit(solution)/shard_map/ra2/ppermute | solution.py:328
  110.5 1.0 copy-done.10
  111.5 9.5 %back_parts.5 = bf16[256,2048]{1,0:T(8,128)(2,1)} custom-call(s32[5]{0:T(128)S(1)} %stack.23.place, bf16[128,4096]{1,0:T(8,128)(2,1)} %copy-done.4, bf16[128,4096]{1,0:T(8,128)(2,1)} %copy-done.10, bf16[4096,2048]{1,0:T(8,128)(2,1)} %refs_3_.3), custom_call_target="tpu_custom_call" | custom-call | flops 1 | bytes 1 | tf_op jit(solution)/shard_map/back_parts/pallas_call | solution.py:220
  121.0 3.5 %collective-permute-start.21 = (bf16[256,2048]{1,0:T(8,128)(2,1)}, bf16[256,2048]{1,0:T(8,128)(2,1)S(1)}, u32[]{:S(2)}, u32[]{:S(2)}) collective-permute-start(bf16[256,2048]{1,0:T(8,128)(2,1)} %back_parts.5), channel_id=1, source_target_pairs={{0,8},{16,24},{1,17},{9,25},{2,10},{18,26},{3,19},{11,27},{28,20},... | collective-permute-start | bytes 3145736 | tf_op jit(solution)/shard_map/l1/ppermute | solution.py:333
  124.5 0.4 add_parts.9
  124.9 7.4 %collective-permute-done.23 = bf16[256,2048]{1,0:T(8,128)(2,1)S(1)} collective-permute-done((bf16[256,2048]{1,0:T(8,128)(2,1)S(1)}, bf16[256,2048]{1,0:T(8,128)(2,1)S(1)}, u32[]{:S(2)}, u32[]{:S(2)}) %collective-permute-start.23) | collective-permute-done | bytes 1048608 | tf_op jit(solution)/shard_map/e1/ppermute | solution.py:333
  132.3 1.6 collective-permute-start.25
  133.9 0.4 add_parts.8
  134.3 3.2 %collective-permute-start.24 = (bf16[128,4096]{1,0:T(8,128)(2,1)S(1)}, bf16[128,4096]{1,0:T(8,128)(2,1)}, u32[]{:S(2)}, u32[]{:S(2)}) collective-permute-start(bf16[128,4096]{1,0:T(8,128)(2,1)S(1)} %add_parts.8), channel_id=1, source_target_pairs={{0,2},{1,3},{2,0},{3,1},{4,6},{5,7},{6,4},{7,5},{8,10},{9,11},{10,... | collective-permute-start | bytes 3145736 | tf_op jit(solution)/shard_map/ra3/ppermute | solution.py:328
  137.5 1.4 add_convert_fusion.1
  138.9 0.5 collective-permute-start.29
  139.4 9.7 %pre_parts.5 = (bf16[128,4096]{1,0:T(8,128)(2,1)S(1)}, bf16[128,2048]{1,0:T(8,128)(2,1)S(1)}, bf16[128,2048]{1,0:T(8,128)(2,1)}) custom-call(s32[5]{0:T(128)S(1)} %stack.23.place, bf16[256,2048]{1,0:T(8,128)(2,1)} %own.7, bf16[256,2048]{1,0:T(8,128)(2,1)} %copy-done.1, bf16[256,2048]{1,0:T(8,128)(2,1)} %copy-done.2, ...), custom_call_target="tpu_custom_call" | custom-call | flops 1 | bytes 1 | tf_op jit(solution)/shard_map/pre_parts/pallas_call | solution.py:136
  149.1 0.1 collective-permute-start.26
  149.2 0.5 collective-permute-start.27
  149.7 1.4 add_convert_fusion
  151.1 0.8 copy-done.17
  151.9 1.6 collective-permute-start.28
  153.5 25.2 %weight_grads.1 = (f32[4096,2048]{1,0:T(8,128)}, f32[1,4096]{1,0:T(1,128)}) custom-call(s32[5]{0:T(128)S(1)} %stack.23.place, bf16[256,2048]{1,0:T(8,128)(2,1)} %own.7, bf16[256,2048]{1,0:T(8,128)(2,1)} %copy-done.1, bf16[256,2048]{1,0:T(8,128)(2,1)} %copy-done.2, bf16[256,2048]{1,0:T(8,128)(2,1)} %collective-permute-done.7.refs_2_, ...), custom_call_target="tpu_custom_call" | custom-call | flops 1 | bytes 1 | tf_op jit(solution)/shard_map/weight_grads/pallas_call | solution.py:260
  178.8 3.8 %fusion.1 = bf16[128,4096]{1,0:T(8,128)(2,1)} fusion(bf16[128,4096]{1,0:T(8,128)(2,1)S(1)} %copy-done.12, bf16[128,4096]{1,0:T(8,128)(2,1)S(1)} %get-tuple-element.100, bf16[128,4096]{1,0:T(8,128)(2,1)} %collective-permute-done.25, bf16[128,4096]{1,0:T(8,128)(2,1)} %collective-permute-done.24, bf16[128,2048]{1,0:T(8,128)(2,1)} %collective-permute-done.27, ...), kind=kLoop, calls=%fused_computation.3 | loop fusion | flops 7340032 | bytes 6307840 | tf_op jit(solution)/shard_map/convert_element_type | solution.py:421
  182.6 3.8 %select_convert_fusion = bf16[256,2048]{1,0:T(8,128)(2,1)} fusion(bf16[256,2048]{1,0:T(8,128)(2,1)} %collective-permute-done.29, bf16[256,2048]{1,0:T(8,128)(2,1)S(1)} %copy-done.16, bf16[256,2048]{1,0:T(8,128)(2,1)S(1)} %copy-done.8, bf16[256,2048]{1,0:T(8,128)(2,1)} %collective-permute-done.28, bf16[256,2048]{1,0:T(8,128)(2,1)} %add_convert_fusion, pred[]{:T(512)S(6)} %eq.29), kind=kLoop, calls=%fused_computation.4 | loop fusion | flops 5242880 | bytes 6291457 | tf_op jit(solution)/shard_map/convert_element_type | solution.py:423
  (58 shorter events, 0.2 us)
Async XLA Ops:
  0.6 16.0 %copy-start = (bf16[256,2048]{1,0:T(8,128)(2,1)S(1)}, bf16[256,2048]{1,0:T(8,128)(2,1)}, u32[]{:S(2)}) copy-start(bf16[256,2048]{1,0:T(8,128)(2,1)} %own.7) | copy-start | bytes 3145732
  0.6 16.0 %collective-permute-start.2 = (bf16[256,2048]{1,0:T(8,128)(2,1)}, bf16[256,2048]{1,0:T(8,128)(2,1)S(1)}, u32[]{:S(2)}, u32[]{:S(2)}) collective-permute-start(bf16[256,2048]{1,0:T(8,128)(2,1)} %own.7), channel_id=1, source_target_pairs={{0,8},{8,0},{16,24},{24,16},{1,17},{9,25},{17,1},{25,9},{2,10},{10... | collective-permute-start | bytes 3145736 | tf_op jit(solution)/shard_map/p1/ppermute | solution.py:333
  5.4 12.7 %copy-start.5 = (bf16[128,4096]{1,0:T(8,128)(2,1)}, bf16[128,4096]{1,0:T(8,128)(2,1)S(1)}, u32[]{:S(2)}) copy-start(bf16[128,4096]{1,0:T(8,128)(2,1)S(1)} %fusion.refs_0_.refs_3_) | copy-start | bytes 3145732
  5.4 15.0 %collective-permute-start.4 = (bf16[128,4096]{1,0:T(8,128)(2,1)S(1)}, bf16[128,4096]{1,0:T(8,128)(2,1)}, u32[]{:S(2)}, u32[]{:S(2)}) collective-permute-start(bf16[128,4096]{1,0:T(8,128)(2,1)S(1)} %fusion.refs_0_.refs_3_), channel_id=1, source_target_pairs={{0,1},{1,0},{2,3},{3,2},{4,5},{5,4},{6,7},{7,6},{8,9},{9,8},{10,11... | collective-permute-start | bytes 3145736 | tf_op jit(solution)/shard_map/h0/ppermute | solution.py:324
  5.5 25.7 %collective-permute-start = (bf16[128,4096]{1,0:T(8,128)(2,1)S(1)}, bf16[128,4096]{1,0:T(8,128)(2,1)}, u32[]{:S(2)}, u32[]{:S(2)}) collective-permute-start(bf16[128,4096]{1,0:T(8,128)(2,1)S(1)} %fusion.refs_0_.refs_3_), channel_id=1, source_target_pairs={{0,2},{1,3},{2,0},{3,1},{4,6},{5,7},{6,4},{7,5},{8,10},{9,11},{10,... | collective-permute-start | bytes 3145736 | tf_op jit(solution)/shard_map/a0/ppermute | solution.py:328
  7.2 24.0 %collective-permute-start.1 = (bf16[128,4096]{1,0:T(8,128)(2,1)S(1)}, bf16[128,4096]{1,0:T(8,128)(2,1)}, u32[]{:S(2)}, u32[]{:S(2)}) collective-permute-start(bf16[128,4096]{1,0:T(8,128)(2,1)S(1)} %fusion.refs_0_.refs_3_), channel_id=1, source_target_pairs={{2,4},{3,5},{4,2},{5,3},{10,12},{11,13},{12,10},{13,11},{18,20},{1... | collective-permute-start | bytes 3145736 | tf_op jit(solution)/shard_map/b0/ppermute | solution.py:328
  16.6 1.7 copy-start.1
  18.3 15.0 %collective-permute-start.3 = (bf16[256,2048]{1,0:T(8,128)(2,1)}, bf16[256,2048]{1,0:T(8,128)(2,1)S(1)}, u32[]{:S(2)}, u32[]{:S(2)}) collective-permute-start(bf16[256,2048]{1,0:T(8,128)(2,1)} %get-tuple-element.115), channel_id=1, source_target_pairs={{0,16},{8,24},{16,0},{24,8},{1,9},{9,1},{17,25},{25,17},{2,18},{10... | collective-permute-start | bytes 3145736 | tf_op jit(solution)/shard_map/p2/ppermute | solution.py:333
  33.3 5.0 %copy-start.2 = (bf16[256,2048]{1,0:T(8,128)(2,1)}, bf16[256,2048]{1,0:T(8,128)(2,1)S(1)}, u32[]{:S(2)}) copy-start(bf16[256,2048]{1,0:T(8,128)(2,1)S(1)} %collective-permute-done.3.refs_1_) | copy-start | bytes 3145732
  33.3 15.1 %collective-permute-start.7 = (bf16[256,2048]{1,0:T(8,128)(2,1)}, bf16[256,2048]{1,0:T(8,128)(2,1)}, u32[]{:S(2)}, u32[]{:S(2)}) collective-permute-start(bf16[256,2048]{1,0:T(8,128)(2,1)} %get-tuple-element.68), channel_id=1, source_target_pairs={{0,16},{8,24},{16,0},{24,8},{1,9},{9,1},{17,25},{25,17},{2,18},{10... | collective-permute-start | bytes 3145736 | tf_op jit(solution)/shard_map/p3/ppermute | solution.py:333
  35.4 38.7 %collective-permute-start.5 = (bf16[128,4096]{1,0:T(8,128)(2,1)}, bf16[128,4096]{1,0:T(8,128)(2,1)}, u32[]{:S(2)}, u32[]{:S(2)}) collective-permute-start(bf16[128,4096]{1,0:T(8,128)(2,1)} %collective-permute-done.1), channel_id=1, source_target_pairs={{2,0},{3,1},{4,6},{5,7},{10,8},{11,9},{12,14},{13,15},{18,16},{19,... | collective-permute-start | bytes 3145736 | tf_op jit(solution)/shard_map/a1/ppermute | solution.py:328
  36.6 37.9 %collective-permute-start.6 = (bf16[128,4096]{1,0:T(8,128)(2,1)}, bf16[128,4096]{1,0:T(8,128)(2,1)}, u32[]{:S(2)}, u32[]{:S(2)}) collective-permute-start(bf16[128,4096]{1,0:T(8,128)(2,1)} %collective-permute-done.refs_0_.refs_5_), channel_id=1, source_target_pairs={{2,4},{3,5},{4,2},{5,3},{10,12},{11,13},{12,10},{13,11},{18,20},{1... | collective-permute-start | bytes 3145736 | tf_op jit(solution)/shard_map/b1/ppermute | solution.py:328
  47.5 2.0 %collective-permute-start.8 = (bf16[128,2048]{1,0:T(8,128)(2,1)S(1)}, bf16[128,2048]{1,0:T(8,128)(2,1)S(1)}, u32[]{:S(2)}, u32[]{:S(2)}) collective-permute-start(bf16[128,2048]{1,0:T(8,128)(2,1)S(1)} %get-tuple-element.70), channel_id=1, source_target_pairs={{0,1},{1,0},{2,3},{3,2},{4,5},{5,4},{6,7},{7,6},{8,9},{9,8},{10,11... | collective-permute-start | bytes 1572872 | tf_op jit(solution)/shard_map/o0/ppermute | solution.py:324
  47.6 2.6 %collective-permute-start.9 = (bf16[128,2048]{1,0:T(8,128)(2,1)S(1)}, bf16[128,2048]{1,0:T(8,128)(2,1)S(1)}, u32[]{:S(2)}, u32[]{:S(2)}) collective-permute-start(bf16[128,2048]{1,0:T(8,128)(2,1)S(1)} %get-tuple-element.71), channel_id=1, source_target_pairs={{0,1},{1,0},{2,3},{3,2},{4,5},{5,4},{6,7},{7,6},{8,9},{9,8},{10,11... | collective-permute-start | bytes 1572872 | tf_op jit(solution)/shard_map/o0/ppermute | solution.py:324
  48.5 39.8 %collective-permute-start.16 = (bf16[128,4096]{1,0:T(8,128)(2,1)}, bf16[128,4096]{1,0:T(8,128)(2,1)S(1)}, u32[]{:S(2)}, u32[]{:S(2)}) collective-permute-start(bf16[128,4096]{1,0:T(8,128)(2,1)} %collective-permute-done.refs_0_.refs_5_), channel_id=1, source_target_pairs={{0,1},{1,0},{2,3},{3,2},{4,5},{5,4},{6,7},{7,6},{8,9},{9,8},{10,11... | collective-permute-start | bytes 3145736 | tf_op jit(solution)/shard_map/h1/ppermute | solution.py:324
  50.5 31.9 %collective-permute-start.11 = (bf16[128,4096]{1,0:T(8,128)(2,1)S(1)}, bf16[128,4096]{1,0:T(8,128)(2,1)S(1)}, u32[]{:S(2)}, u32[]{:S(2)}) collective-permute-start(bf16[128,4096]{1,0:T(8,128)(2,1)S(1)} %add_parts.5), channel_id=1, source_target_pairs={{0,2},{1,3},{6,4},{7,5},{8,10},{9,11},{14,12},{15,13},{16,18},{17,... | collective-permute-start | bytes 3145736 | tf_op jit(solution)/shard_map/ra1/ppermute | solution.py:328
  74.0 2.1 %collective-permute-start.12 = (bf16[128,2048]{1,0:T(8,128)(2,1)S(1)}, bf16[128,2048]{1,0:T(8,128)(2,1)S(1)}, u32[]{:S(2)}, u32[]{:S(2)}) collective-permute-start(bf16[128,2048]{1,0:T(8,128)(2,1)S(1)} %get-tuple-element.78), channel_id=1, source_target_pairs={{0,1},{1,0},{2,3},{3,2},{4,5},{5,4},{6,7},{7,6},{8,9},{9,8},{10,11... | collective-permute-start | bytes 1572872 | tf_op jit(solution)/shard_map/o1/ppermute | solution.py:324
  74.1 3.3 %collective-permute-start.13 = (bf16[128,2048]{1,0:T(8,128)(2,1)S(1)}, bf16[128,2048]{1,0:T(8,128)(2,1)S(1)}, u32[]{:S(2)}, u32[]{:S(2)}) collective-permute-start(bf16[128,2048]{1,0:T(8,128)(2,1)S(1)} %get-tuple-element.79), channel_id=1, source_target_pairs={{0,1},{1,0},{2,3},{3,2},{4,5},{5,4},{6,7},{7,6},{8,9},{9,8},{10,11... | collective-permute-start | bytes 1572872 | tf_op jit(solution)/shard_map/o1/ppermute | solution.py:324
  75.9 7.1 %copy-start.3 = (bf16[128,4096]{1,0:T(8,128)(2,1)}, bf16[128,4096]{1,0:T(8,128)(2,1)S(1)}, u32[]{:S(2)}) copy-start(bf16[128,4096]{1,0:T(8,128)(2,1)S(1)} %broadcast_select_fusion.1.refs_2_.refs_7_) | copy-start | bytes 3145732
  75.9 12.3 %collective-permute-start.17 = (bf16[128,4096]{1,0:T(8,128)(2,1)S(1)}, bf16[128,4096]{1,0:T(8,128)(2,1)S(1)}, u32[]{:S(2)}, u32[]{:S(2)}) collective-permute-start(bf16[128,4096]{1,0:T(8,128)(2,1)S(1)} %broadcast_select_fusion.1.refs_2_.refs_7_), channel_id=1, source_target_pairs={{0,1},{1,0},{2,3},{3,2},{4,5},{5,4},{6,7},{7,6},{8,9},{9,8},{10,11... | collective-permute-start | bytes 3145736 | tf_op jit(solution)/shard_map/h2/ppermute | solution.py:324
  76.1 28.7 %collective-permute-start.10 = (bf16[128,4096]{1,0:T(8,128)(2,1)}, bf16[128,4096]{1,0:T(8,128)(2,1)S(1)}, u32[]{:S(2)}, u32[]{:S(2)}) collective-permute-start(bf16[128,4096]{1,0:T(8,128)(2,1)} %collective-permute-done.6), channel_id=1, source_target_pairs={{2,0},{3,1},{4,6},{5,7},{10,8},{11,9},{12,14},{13,15},{18,16},{19,... | collective-permute-start | bytes 3145736 | tf_op jit(solution)/shard_map/a2/ppermute | solution.py:328
  77.4 5.6 %collective-permute-start.14 = (bf16[128,2048]{1,0:T(8,128)(2,1)S(1)}, bf16[128,2048]{1,0:T(8,128)(2,1)S(1)}, u32[]{:S(2)}, u32[]{:S(2)}) collective-permute-start(bf16[128,2048]{1,0:T(8,128)(2,1)S(1)} %get-tuple-element.80), channel_id=1, source_target_pairs={{0,1},{1,0},{2,3},{3,2},{4,5},{5,4},{6,7},{7,6},{8,9},{9,8},{10,11... | collective-permute-start | bytes 1572872 | tf_op jit(solution)/shard_map/o2/ppermute | solution.py:324
  82.4 5.1 %collective-permute-start.15 = (bf16[128,2048]{1,0:T(8,128)(2,1)S(1)}, bf16[128,2048]{1,0:T(8,128)(2,1)S(1)}, u32[]{:S(2)}, u32[]{:S(2)}) collective-permute-start(bf16[128,2048]{1,0:T(8,128)(2,1)S(1)} %get-tuple-element.81), channel_id=1, source_target_pairs={{0,1},{1,0},{2,3},{3,2},{4,5},{5,4},{6,7},{7,6},{8,9},{9,8},{10,11... | collective-permute-start | bytes 1572872 | tf_op jit(solution)/shard_map/o2/ppermute | solution.py:324
  83.0 27.5 %collective-permute-start.19 = (bf16[128,4096]{1,0:T(8,128)(2,1)S(1)}, bf16[128,4096]{1,0:T(8,128)(2,1)S(1)}, u32[]{:S(2)}, u32[]{:S(2)}) collective-permute-start(bf16[128,4096]{1,0:T(8,128)(2,1)S(1)} %add_parts.7), channel_id=1, source_target_pairs={{0,2},{1,3},{6,4},{7,5},{8,10},{9,11},{14,12},{15,13},{16,18},{17,... | collective-permute-start | bytes 3145736 | tf_op jit(solution)/shard_map/ra2/ppermute | solution.py:328
  87.5 23.0 %collective-permute-start.18 = (bf16[128,4096]{1,0:T(8,128)(2,1)S(1)}, bf16[128,4096]{1,0:T(8,128)(2,1)S(1)}, u32[]{:S(2)}, u32[]{:S(2)}) collective-permute-start(bf16[128,4096]{1,0:T(8,128)(2,1)S(1)} %add_parts.6), channel_id=1, source_target_pairs={{2,4},{3,5},{4,2},{5,3},{10,12},{11,13},{12,10},{13,11},{18,20},{1... | collective-permute-start | bytes 3145736 | tf_op jit(solution)/shard_map/rb2/ppermute | solution.py:328
  88.3 1.0 copy-start.6
  89.2 1.0 copy-start.7
  104.7 1.6 copy-start.14
  104.7 3.0 %copy-start.13 = (bf16[256,2048]{1,0:T(8,128)(2,1)S(1)}, bf16[256,2048]{1,0:T(8,128)(2,1)}, u32[]{:S(2)}) copy-start(bf16[256,2048]{1,0:T(8,128)(2,1)} %get-tuple-element.94) | copy-start | bytes 3145732
  104.9 5.6 %copy-start.4 = (bf16[128,4096]{1,0:T(8,128)(2,1)}, bf16[128,4096]{1,0:T(8,128)(2,1)S(1)}, u32[]{:S(2)}) copy-start(bf16[128,4096]{1,0:T(8,128)(2,1)S(1)} %broadcast_select_fusion.refs_0_.refs_9_) | copy-start | bytes 3145732
  104.9 5.6 %collective-permute-start.20 = (bf16[128,4096]{1,0:T(8,128)(2,1)S(1)}, bf16[128,4096]{1,0:T(8,128)(2,1)S(1)}, u32[]{:S(2)}, u32[]{:S(2)}) collective-permute-start(bf16[128,4096]{1,0:T(8,128)(2,1)S(1)} %broadcast_select_fusion.refs_0_.refs_9_), channel_id=1, source_target_pairs={{0,1},{1,0},{2,3},{3,2},{4,5},{5,4},{6,7},{7,6},{8,9},{9,8},{10,11... | collective-permute-start | bytes 3145736 | tf_op jit(solution)/shard_map/h3/ppermute | solution.py:324
  106.3 18.6 %collective-permute-start.22 = (bf16[256,2048]{1,0:T(8,128)(2,1)S(1)}, bf16[256,2048]{1,0:T(8,128)(2,1)S(1)}, u32[]{:S(2)}, u32[]{:S(2)}) collective-permute-start(bf16[256,2048]{1,0:T(8,128)(2,1)S(1)} %copy-done.14), channel_id=1, source_target_pairs={{0,8},{8,0},{16,24},{24,16},{1,17},{9,25},{17,1},{25,9},{2,10},{10... | collective-permute-start | bytes 3145736 | tf_op jit(solution)/shard_map/f1/ppermute | solution.py:333
  107.8 24.5 %collective-permute-start.23 = (bf16[256,2048]{1,0:T(8,128)(2,1)S(1)}, bf16[256,2048]{1,0:T(8,128)(2,1)S(1)}, u32[]{:S(2)}, u32[]{:S(2)}) collective-permute-start(bf16[256,2048]{1,0:T(8,128)(2,1)S(1)} %copy-done.13), channel_id=1, source_target_pairs={{0,8},{8,0},{16,24},{24,16},{1,17},{9,25},{17,1},{25,9},{2,10},{10... | collective-permute-start | bytes 3145736 | tf_op jit(solution)/shard_map/e1/ppermute | solution.py:333
  110.5 1.0 copy-start.10
  121.0 28.2 %collective-permute-start.21 = (bf16[256,2048]{1,0:T(8,128)(2,1)}, bf16[256,2048]{1,0:T(8,128)(2,1)S(1)}, u32[]{:S(2)}, u32[]{:S(2)}) collective-permute-start(bf16[256,2048]{1,0:T(8,128)(2,1)} %back_parts.5), channel_id=1, source_target_pairs={{0,8},{16,24},{1,17},{9,25},{2,10},{18,26},{3,19},{11,27},{28,20},... | collective-permute-start | bytes 3145736 | tf_op jit(solution)/shard_map/l1/ppermute | solution.py:333
  132.3 2.0 %copy-start.15 = (bf16[256,2048]{1,0:T(8,128)(2,1)}, bf16[256,2048]{1,0:T(8,128)(2,1)S(1)}, u32[]{:S(2)}) copy-start(bf16[256,2048]{1,0:T(8,128)(2,1)S(1)} %collective-permute-done.23) | copy-start | bytes 3145732
  132.3 46.5 %collective-permute-start.25 = (bf16[128,4096]{1,0:T(8,128)(2,1)S(1)}, bf16[128,4096]{1,0:T(8,128)(2,1)}, u32[]{:S(2)}, u32[]{:S(2)}) collective-permute-start(bf16[128,4096]{1,0:T(8,128)(2,1)S(1)} %add_parts.9), channel_id=1, source_target_pairs={{2,4},{3,5},{4,2},{5,3},{10,12},{11,13},{12,10},{13,11},{18,20},{1... | collective-permute-start | bytes 3145736 | tf_op jit(solution)/shard_map/rb3/ppermute | solution.py:328
  133.9 3.6 %copy-start.9 = (bf16[256,2048]{1,0:T(8,128)(2,1)S(1)}, bf16[256,2048]{1,0:T(8,128)(2,1)}, u32[]{:S(2)}) copy-start(bf16[256,2048]{1,0:T(8,128)(2,1)} %get-tuple-element.92) | copy-start | bytes 3145732
  134.3 44.5 %collective-permute-start.24 = (bf16[128,4096]{1,0:T(8,128)(2,1)S(1)}, bf16[128,4096]{1,0:T(8,128)(2,1)}, u32[]{:S(2)}, u32[]{:S(2)}) collective-permute-start(bf16[128,4096]{1,0:T(8,128)(2,1)S(1)} %add_parts.8), channel_id=1, source_target_pairs={{0,2},{1,3},{2,0},{3,1},{4,6},{5,7},{6,4},{7,5},{8,10},{9,11},{10,... | collective-permute-start | bytes 3145736 | tf_op jit(solution)/shard_map/ra3/ppermute | solution.py:328
  138.9 10.8 %copy-start.11 = (bf16[256,2048]{1,0:T(8,128)(2,1)S(1)}, bf16[256,2048]{1,0:T(8,128)(2,1)}, u32[]{:S(2)}) copy-start(bf16[256,2048]{1,0:T(8,128)(2,1)} %back_parts.5) | copy-start | bytes 3145732
  138.9 43.7 %collective-permute-start.29 = (bf16[256,2048]{1,0:T(8,128)(2,1)}, bf16[256,2048]{1,0:T(8,128)(2,1)}, u32[]{:S(2)}, u32[]{:S(2)}) collective-permute-start(bf16[256,2048]{1,0:T(8,128)(2,1)} %add_convert_fusion.1), channel_id=1, source_target_pairs={{0,16},{8,24},{16,0},{24,8},{1,9},{9,1},{17,25},{25,17},{2,18},{10... | collective-permute-start | bytes 3145736 | tf_op jit(solution)/shard_map/e2/ppermute | solution.py:333
  149.1 4.4 %copy-start.19 = (bf16[4096]{0:T(1024)(128)(2,1)S(1)}, bf16[4096]{0:T(1024)(128)(2,1)}, u32[]{:S(2)}) copy-start(bf16[4096]{0:T(1024)(128)(2,1)} %param.9) | copy-start | bytes 24580
  149.1 2.0 %collective-permute-start.26 = (bf16[128,2048]{1,0:T(8,128)(2,1)S(1)}, bf16[128,2048]{1,0:T(8,128)(2,1)S(1)}, u32[]{:S(2)}, u32[]{:S(2)}) collective-permute-start(bf16[128,2048]{1,0:T(8,128)(2,1)S(1)} %get-tuple-element.105), channel_id=1, source_target_pairs={{0,1},{1,0},{2,3},{3,2},{4,5},{5,4},{6,7},{7,6},{8,9},{9,8},{10,11... | collective-permute-start | bytes 1572872 | tf_op jit(solution)/shard_map/o3/ppermute | solution.py:324
  149.2 29.6 %collective-permute-start.27 = (bf16[128,2048]{1,0:T(8,128)(2,1)}, bf16[128,2048]{1,0:T(8,128)(2,1)}, u32[]{:S(2)}, u32[]{:S(2)}) collective-permute-start(bf16[128,2048]{1,0:T(8,128)(2,1)} %get-tuple-element.106), channel_id=1, source_target_pairs={{0,1},{1,0},{2,3},{3,2},{4,5},{5,4},{6,7},{7,6},{8,9},{9,8},{10,11... | collective-permute-start | bytes 1572872 | tf_op jit(solution)/shard_map/o3/ppermute | solution.py:324
  151.1 0.8 copy-start.17
  151.9 30.7 %collective-permute-start.28 = (bf16[256,2048]{1,0:T(8,128)(2,1)}, bf16[256,2048]{1,0:T(8,128)(2,1)}, u32[]{:S(2)}, u32[]{:S(2)}) collective-permute-start(bf16[256,2048]{1,0:T(8,128)(2,1)} %add_convert_fusion), channel_id=1, source_target_pairs={{8,24},{17,25},{10,26},{19,27},{20,4},{13,5},{22,6},{15,7}} | collective-permute-start | bytes 3145736 | tf_op jit(solution)/shard_map/l2/ppermute | solution.py:333
  153.5 25.3 %copy-start.12 = (bf16[128,4096]{1,0:T(8,128)(2,1)S(1)}, bf16[128,4096]{1,0:T(8,128)(2,1)}, u32[]{:S(2)}) copy-start(bf16[128,4096]{1,0:T(8,128)(2,1)} %param.7) | copy-start | bytes 3145732
  153.5 25.3 %copy-start.18 = (bf16[128,2048]{1,0:T(8,128)(2,1)S(1)}, bf16[128,2048]{1,0:T(8,128)(2,1)}, u32[]{:S(2)}) copy-start(bf16[128,2048]{1,0:T(8,128)(2,1)} %copy-done.17) | copy-start | bytes 1572868
  178.8 3.8 %copy-start.8 = (bf16[256,2048]{1,0:T(8,128)(2,1)S(1)}, bf16[256,2048]{1,0:T(8,128)(2,1)}, u32[]{:S(2)}) copy-start(bf16[256,2048]{1,0:T(8,128)(2,1)} %get-tuple-element.87) | copy-start | bytes 3145732
  178.8 3.8 %copy-start.16 = (bf16[256,2048]{1,0:T(8,128)(2,1)S(1)}, bf16[256,2048]{1,0:T(8,128)(2,1)}, u32[]{:S(2)}) copy-start(bf16[256,2048]{1,0:T(8,128)(2,1)} %copy-done.15) | copy-start | bytes 3145732

commit v2 on v1

--- a/solution.py
+++ b/solution.py
@@ -64,8 +64,15 @@
 
 def pre_block(place, index):
     middle = jnp.logical_or(place[Z] == 1, place[Z] == 2)
-    rel = {0: 0, 1: 1, 2: jnp.where(middle, 3, 2), 3: jnp.where(middle, 2, 3)}[index]
-    return rel ^ place[FIRST]
+    swapped = jnp.where(index == 2, 3, jnp.where(index == 3, 2, index))
+    return jnp.where(middle, swapped, index) ^ place[FIRST]
+
+
+def pre_order(place):
+    middle = jnp.logical_or(place[Z] == 1, place[Z] == 2)
+    rel = place[REL]
+    own = jnp.where(middle, jnp.where(rel == 2, 3, jnp.where(rel == 3, 2, rel)), rel)
+    return own, jnp.where(own == 0, 1, 0), jnp.where(own <= 1, 2, 1), jnp.where(own == 3, 2, 3)
 
 
 def back_block(place, slot):
@@ -73,14 +80,14 @@
     return (place[Z], place[Z] ^ 1, jnp.where(low, 2, 1), jnp.where(low, 3, 0))[slot]
 
 
-def pre_kernel(indices, n_got, chunks, place, own, *refs):
+def pre_kernel(turns, slots, n_got, n_prior, chunks, place, own, *refs):
     got = list(refs[:n_got]) + [None] * (3 - n_got)
-    w, refs = refs[n_got], refs[n_got + 1 :]
-    n_out = 2 * len(indices)
-    n_ref = (1 + PIECES) * len(indices)
-    outs, (held, held_w, held_y, sem, sem_w, sem_y) = refs[:n_ref], refs[n_ref:]
+    w, refs = refs[n_got], refs[n_got + 1 + n_prior :]
+    outs, (held, held_w, held_y, sem, sem_w, sem_y) = refs[:-6], refs[-6:]
     lanes = held.shape[1]
     tile = w.shape[0] // chunks
+    run = chunks // PIECES
+    order = pre_order(place)
 
     def w_copy(i):
         part = pl.ds(pl.multiple_of(i * tile, tile), tile)
@@ -91,30 +98,34 @@
         return pltpu.make_async_copy(held_y.at[i, pl.ds(k * lanes, lanes)], out.at[:, part], sem_y.at[i, k])
 
     def start_y(i):
-        run = chunks // PIECES
-        for b in range(len(indices)):
-            mine, *other = outs[(1 + PIECES) * b : (1 + PIECES) * (b + 1)]
-            y_copy(i, 2 * b, mine, i).start()
-            for piece, out in enumerate(other):
-
-                @pl.when(i // run == piece)
+        for b, turn in enumerate(turns):
+            for at, slot in enumerate(slots):
+                mine, *other = outs[(1 + PIECES) * at : (1 + PIECES) * (at + 1)]
+
+                @pl.when(order[turn] == slot)
                 def _():
-                    y_copy(i, 2 * b + 1, out, i % run).start()
-
-    for i, index in enumerate(indices):
-        load_x(place, pre_block(place, index), own, got, held, 2 * i, sem)
+                    y_copy(i, 2 * b, mine, i).start()
+
+                for piece, out in enumerate(other):
+
+                    @pl.when(jnp.logical_and(order[turn] == slot, i // run == piece))
+                    def _():
+                        y_copy(i, 2 * b + 1, out, i % run).start()
+
+    for b, turn in enumerate(turns):
+        load_x(place, pre_block(place, order[turn]), own, got, held, 2 * b, sem)
 
     def start(i, _):
         w_copy(i).start()
         return _
 
     lax.fori_loop(0, chunks, start, 0)
-    for i in range(len(indices)):
-        wait_x(own, held, 2 * i, sem)
+    for b in range(len(turns)):
+        wait_x(own, held, 2 * b, sem)
 
     def step(i, _):
         w_copy(i).wait()
-        x = held[...].reshape(n_out * lanes, held.shape[2])
+        x = held[...].reshape(2 * len(turns) * lanes, held.shape[2])
         rows = held_w[pl.ds(pl.multiple_of(i * tile, tile), tile)]
         held_y[i] = lax.dot_general(x, rows, (((1,), (1,)), ((), ())), preferred_element_type=F32).astype(BF16)
         start_y(i)
@@ -123,34 +134,34 @@
     lax.fori_loop(0, chunks, step, 0)
 
     def finish(i, _):
-        for k in range(n_out):
+        for k in range(2 * len(turns)):
             y_copy(i, k, outs[0], 0).wait()
         return _
 
     lax.fori_loop(0, chunks, finish, 0)
 
 
-def pre_parts(place, own, got, w, indices, chunks):
+def pre_parts(place, own, got, w, turns, slots, chunks, prior=()):
     rows, depth = own.shape
-    lanes, wide, outs = rows // 2, w.shape[0], 2 * len(indices)
-    return pl.pallas_call(
-        functools.partial(pre_kernel, tuple(indices), len(got), chunks),
-        in_specs=[SMEM] + [ANY] * (2 + len(got)),
-        out_specs=[ANY] * ((1 + PIECES) * len(indices)),
+    lanes, wide, parts = rows // 2, w.shape[0], 2 * len(turns)
+    return pl.pallas_call(
+        functools.partial(pre_kernel, turns, slots, len(got), len(prior), chunks),
+        in_specs=[SMEM] + [ANY] * (2 + len(got) + len(prior)),
+        out_specs=[ANY] * ((1 + PIECES) * len(slots)),
         scratch_shapes=[
-            pltpu.VMEM((outs, lanes, depth), BF16),
+            pltpu.VMEM((parts, lanes, depth), BF16),
             pltpu.VMEM((wide, depth), BF16),
-            pltpu.VMEM((chunks, outs * lanes, wide // chunks), BF16),
-            DMA((outs,)),
+            pltpu.VMEM((chunks, parts * lanes, wide // chunks), BF16),
+            DMA((parts,)),
             DMA((chunks,)),
-            DMA((chunks, outs)),
+            DMA((chunks, parts)),
         ],
-        out_shape=[jax.ShapeDtypeStruct((lanes, n), BF16) for n in [wide] + [wide // PIECES] * PIECES]
-        * len(indices),
+        out_shape=[pltpu.HBM((lanes, n), BF16) for n in [wide] + [wide // PIECES] * PIECES] * len(slots),
+        input_output_aliases={3 + len(got) + k: k for k in range(len(prior))},
         compiler_params=params(28),
-        cost_estimate=cost(2 * outs * lanes * depth * wide, 2 * wide * depth),
+        cost_estimate=cost(2 * parts * lanes * depth * wide, 2 * wide * depth),
         name="pre_parts",
-    )(place, *in_hbm(own, *got, w))
+    )(place, *in_hbm(own, *got, w, *prior))
 
 
 def back_kernel(slots, by_role, n_prior, chunks, place, *refs):
@@ -264,9 +275,9 @@
         + [ANY] * 4
         + [pl.BlockSpec((lanes, tile), lambda i: (0, first + i))] * n_h
         + [ANY] * len(prior),
-        out_specs=[pl.BlockSpec((tile, wide), lambda i: (first + i, 0)), pl.BlockSpec((1, tile), lambda i: (0, i))],
+        out_specs=[pl.BlockSpec((tile, wide), lambda i: (first + i, 0)), pl.BlockSpec((1, tile), lambda i: (0, first + i))],
         scratch_shapes=[pltpu.VMEM((n_h, lanes, wide), BF16), DMA((n_h,))],
-        out_shape=[pltpu.HBM((feats, wide), F32), jax.ShapeDtypeStruct((1, count * tile), F32)],
+        out_shape=[pltpu.HBM((feats, wide), F32), pltpu.HBM((1, feats), F32)],
         input_output_aliases={5 + n_h + k: k for k in range(len(prior))},
         compiler_params=params(26),
         cost_estimate=cost(2 * n_h * lanes * wide * feats, 4 * wide * feats),
@@ -303,6 +314,46 @@
     )(q, *more, *pieces)
 
 
+def pair_kernel(a, b, out):
+    out[...] = (a[...].astype(F32) + b[...].astype(F32)).astype(out.dtype)
+
+
+def add_pair(a, b):
+    return pl.pallas_call(
+        pair_kernel,
+        in_specs=[VMEM] * 2,
+        out_specs=VMEM,
+        out_shape=jax.ShapeDtypeStruct(a.shape, BF16),
+        compiler_params=params(8),
+        cost_estimate=cost(0, 0),
+        name="add_pair",
+    )(a, b)
+
+
+def base_kernel(grad, bias, q, *refs):
+    pieces, wide, out = refs[:PIECES], refs[PIECES:-1], refs[-1]
+    run = pieces[0].shape[1]
+    for k, piece in enumerate(pieces):
+        part = pl.ds(k * run, run)
+        total = q[:, part].astype(F32) + piece[...].astype(F32)
+        for ref in wide:
+            total += ref[:, part].astype(F32)
+        total += bias[:, part].astype(F32)
+        out[:, part] = (grad[:, part].astype(F32) * total).astype(out.dtype)
+
+
+def base_grads(grad, bias, q, pieces, *more):
+    return pl.pallas_call(
+        base_kernel,
+        in_specs=[VMEM] * (3 + len(pieces) + len(more)),
+        out_specs=VMEM,
+        out_shape=jax.ShapeDtypeStruct(grad.shape, BF16),
+        compiler_params=params(16),
+        cost_estimate=pl.CostEstimate(flops=1, bytes_accessed=grad.size, transcendentals=0),
+        name="base_grads",
+    )(grad, bias[None, :], q, *pieces, *more)
+
+
 def line_pairs(hops):
     return [(2 * a + core, 2 * b + core) for a, b in hops for core in (0, 1)]
 
@@ -342,10 +393,8 @@
     outwards, inwards = [(1, 0), (2, 3)], [(0, 1), (3, 2)]
 
     cross_weight = pltpu.with_memory_space_constraint(cross_weight, pltpu.VMEM)
-    def pre(indices, got, *done):
-        out = pre_parts(after(place, *done), layer_input, got, cross_weight, indices, 8)
-        each = 1 + PIECES
-        return [part for k in range(len(indices)) for part in (out[each * k], out[each * k + 1 : each * (k + 1)])]
+    def pre(turns, slots, got, *done, prior=()):
+        return list(pre_parts(after(place, *done), layer_input, got, cross_weight, turns, slots, 8, prior))
 
     def back(slots, hs, *done, prior=None, by_role=True):
         return back_parts(after(place, *done), slots, hs, cross_weight, 8, prior, by_role)
@@ -358,6 +407,9 @@
     own_h = (out_grad.astype(F32) * base_input.astype(F32)).astype(BF16)
     a0, b0 = line(own_h, outer, "a0"), line(own_h, inner, "b0")
     h0 = across(own_h, "h0")
+    each = 1 + PIECES
+    q = pre((0,), (0, 1, 2, 3), (), own_h)
+    p1 = after(p1, q[0])
     to_p2 = jnp.where(relays, p1, layer_input)
     to_p3 = jnp.where(relays, layer_input, p1)
     p2 = plane(to_p2, second_way, "p2")
@@ -367,12 +419,13 @@
     a1, b1 = line(b0, outwards, "a1"), line(a0, inner, "b1")
     p3 = plane(to_p3, second_way, "p3")
     h1 = across(a0, "h1")
-    q0, o0 = pre((0,), (p1, p2))
-    o0 = across(o0, "o0")
+    q[: 2 * each] = pre((1,), (0, 1), (p1, p2), prior=q[: 2 * each])
+    q0, o0 = q[0], across(q[1:each], "o0")
     to_ra1 = add_parts(after(q0, p3), o0)
     ra1 = line(to_ra1, inwards, "ra1")
-    q1, o1, q2, o2 = pre((1, 2), (p1, p2, p3), to_ra1)
-    o1, o2 = across(o1, "o1"), across(o2, "o2")
+    q[each:] = pre((2, 3), (1, 2, 3), (p1, p2, p3), to_ra1, prior=q[each:])
+    q1, q2, q3 = q[each], q[2 * each], q[3 * each]
+    o1, o2, o3 = [across(q[k * each + 1 : (k + 1) * each], f"o{k}") for k in (1, 2, 3)]
 
     a1, b1 = both(a1, b1, done=(q1,))
     a2 = line(b1, outwards, "a2")
@@ -387,40 +440,26 @@
     a2, *roles = both(a2, *roles, done=())
     s3 = jnp.where(end, a2, b1)
     h3 = across(s3, "h3")
-    e1, f1 = plane(roles[1], first_way, "e1"), plane(roles[3], first_way, "f1")
     rb2, ra2 = both(rb2, ra2, done=(s3,))
-    (part,) = back((3,), (s3, h3), roles[0], rb2, ra2, by_role=False)
-
-    rb2, ra2 = both(rb2, ra2, done=(part,))
+    mine, near, relayed, far = back((3,), (s3, h3), rb2, ra2, prior=roles)
+
+    rb2, ra2 = both(rb2, ra2, done=(far,))
     to_ra3, to_rb3 = add_parts(q2, o2, rb2), add_parts(q1, o1, ra2)
     ra3, rb3 = line(to_ra3, outer, "ra3"), line(to_rb3, inner, "rb3")
 
-    mine, relayed = roles[0], roles[2]
-    last_of = [3, 3, 0, 0]
-
-    def last_first(k):
-        return [(0, f ^ last_of[k], t ^ last_of[k]) for f, t in ((3, 2), (1, 0))] + [
-            (1, f ^ last_of[k], t ^ last_of[k]) for f, t in ((3, 1), (2, 0))
-        ]
-
-    def last_second(k):
-        return [(0, 2 ^ last_of[k], last_of[k]), (1, 1 ^ last_of[k], last_of[k])]
-
-    l1 = plane(part, last_first, "l1")
-    f1, e1 = both(f1, e1, done=(part,))
-    to_e2 = wide_sum(relayed, f1).astype(BF16)
+    f1, e1 = plane(far, first_way, "f1"), plane(near, first_way, "e1")
+    hs = (own_h, h0, a0, h1, s2, h2, s3, h3)
+    tile = 512
+    tiles = base_input.shape[1] // tile
+    early = tiles * 3 // 4
+    got = (p1, p2, p3)
+    grads = weight_grads(after(place, to_ra3, to_rb3), layer_input, got, hs, tile, 0, early)
+    to_e2 = add_pair(relayed, after(f1, *grads))
     e2 = plane(to_e2, second_way, "e2")
-    q3, o3 = pre((3,), (p1, p2, p3), to_e2, to_ra3, to_rb3)
-    o3 = across(o3, "o3")
-    to_l2 = wide_sum(part, after(l1, q3)).astype(BF16)
-    l2 = plane(to_l2, last_second, "l2")
-    hs = (own_h, h0, a0, h1, s2, h2, s3, h3)
-    grad, bias = weight_grads(after(place, to_l2), layer_input, (p1, p2, p3), hs, 512, 0, base_input.shape[1] // 512)
-    ra3, rb3, *o3 = both(ra3, rb3, *o3, done=(bias,))
-    preact = wide_sum(ra3, rb3, q3, o3) + cross_bias.astype(F32)[None, :]
-    base_grad = (out_grad.astype(F32) * preact).astype(BF16)
-    l2, e2 = both(l2, e2, done=(base_grad,))
-    branch = jnp.where(row == back_block(place, 3), wide_sum(to_l2, l2), wide_sum(mine, e1, e2)).astype(BF16)
+    grad, bias = weight_grads(after(place, to_e2), layer_input, got, hs, tile, early, tiles - early, grads)
+    ra3, rb3, e1, *o3 = both(ra3, rb3, e1, *o3, done=(bias,))
+    base_grad = base_grads(out_grad, cross_bias, q3, o3, ra3, rb3)
+    branch = wide_sum(mine, e1, after(e2, base_grad)).astype(BF16)
     return (grad, bias[0], base_grad, branch)
 
 

time: 188 us -> 169 us (0.90)
  waiting for transfers between devices: 27.5 us -> 17.7 us
  other arithmetic: 15 us -> 6.06 us
  Pallas kernels: 93.5 us -> 101 us
  starting transfers between devices: 44.2 us -> 38.1 us
    ppermute x8 -> x6, waiting for transfers between devices: 17.7 us -> 5.73 us  [plane(): return lax.ppermute(a, ('row', 'col'), pairs)]
    convert_element_type x5 -> x1, other arithmetic: 10.3 us -> 1.51 us  [on_line(): branch = wide_sum(mine, e1, after(e2, base_grad)).astype(BF16)]
    ppermute x8 -> x6, starting transfers between devices: 14.7 us -> 8.55 us  [plane(): return lax.ppermute(a, ('row', 'col'), pairs)]
    pallas_call x1 -> x2, Pallas kernels: 25.2 us -> 30.7 us  [weight_grads(): pl.pallas_call(functools.partial(weight_kernel, n_h, len(prior)), grid=(c...]
    ppermute x10, waiting for transfers between devices: 7.94 us -> 10.1 us  [line(): return lax.ppermute(a, 'col', line_pairs(hops))]
    pallas_call x3 -> x5, Pallas kernels: 33.1 us -> 35.2 us  [the longest x3 33.2 us: pre_parts(): pl.pallas_call(functools.partial(pre_kernel, turns, slots, len(got), len(...]
    unnamed x40 -> x48, local copies, waits for them, and re-layouts: 4.99 us -> 4.49 us
  transfers between devices with their start and end apart: 30 -> 28, of which waited for: 9 -> 9; matrix products, arithmetic and copies ran while one was open for 6% -> 3% of each run, Pallas kernels for 50% -> 54%
where the time goes in v2:
time: 169 us; the launch traced here: 168 us
  Pallas kernels  101 us (60%)
  starting transfers between devices  38.1 us (23%)
  waiting for transfers between devices  17.7 us (10%)
  other arithmetic  6.06 us (4%)
  local copies, waits for them, and re-layouts  4.59 us (3%)
    pallas_call x3, Pallas kernels, pre_parts(): pl.pallas_call(functools.partial(pre_kernel, turns, slots, len(got), len(...  33.2 us
    pallas_call x3, Pallas kernels, back_parts(): pl.pallas_call(functools.partial(back_kernel, tuple(slots), by_role, len(...  33.1 us
    pallas_call x2, Pallas kernels, weight_grads(): pl.pallas_call(functools.partial(weight_kernel, n_h, len(prior)), grid=(c...  30.7 us
    ppermute x10, starting transfers between devices, line(): return lax.ppermute(a, 'col', line_pairs(hops))  27.5 us
    ppermute x10, waiting for transfers between devices, line(): return lax.ppermute(a, 'col', line_pairs(hops))  10.1 us
    ppermute x6, starting transfers between devices, plane(): return lax.ppermute(a, ('row', 'col'), pairs)  8.55 us
    ppermute x6, waiting for transfers between devices, plane(): return lax.ppermute(a, ('row', 'col'), pairs)  5.73 us
    unnamed x48, local copies, waits for them, and re-layouts  4.49 us
  transfers between devices with their start and end apart: 28, of which 9 were waited for; matrix products, arithmetic and copies ran while one was open for 3% of the time, Pallas kernels for 54%

profile of v2, /device:TPU:0, one launch (start us, length us, event | category | flops | bytes accessed | tf_op | source)
XLA Modules:
  0.0 168.2 jit_solution(11391780184814848670)
XLA Ops:
  0.6 3.0 %collective-permute-start = (bf16[256,2048]{1,0:T(8,128)(2,1)}, bf16[256,2048]{1,0:T(8,128)(2,1)S(1)}, u32[]{:S(2)}, u32[]{:S(2)}) collective-permute-start(bf16[256,2048]{1,0:T(8,128)(2,1)} %own.9), channel_id=1, source_target_pairs={{0,8},{8,0},{16,24},{24,16},{1,17},{9,25},{17,1},{25,9},{2,10},{10... | collective-permute-start | bytes 3145736 | tf_op jit(solution)/shard_map/p1/ppermute | solution.py:384
  3.6 1.8 %multiply_convert_fusion.refs_0_.refs_3_ = bf16[128,4096]{1,0:T(8,128)(2,1)S(1)} fusion(bf16[128,4096]{1,0:T(8,128)(2,1)} %param.5, bf16[128,4096]{1,0:T(8,128)(2,1)} %grad.1), kind=kLoop, calls=%fused_computation.1 | loop fusion | flops 2097152 | bytes 3145728 | tf_op jit(solution)/shard_map/convert_element_type | solution.py:407
  5.4 0.1 collective-permute-start.4
  5.5 1.6 collective-permute-start.1
  7.2 1.7 collective-permute-start.2
  8.8 0.1 stack.23.place
  8.9 9.4 %pre_parts.3 = (bf16[128,4096]{1,0:T(8,128)(2,1)}, bf16[128,2048]{1,0:T(8,128)(2,1)}, bf16[128,2048]{1,0:T(8,128)(2,1)}, bf16[128,4096]{1,0:T(8,128)(2,1)}, bf16...) custom-call(s32[5]{0:T(128)S(1)} %stack.23.place, ...), custom_call_target="tpu_custom_call" | custom-call | flops 1 | bytes 1 | tf_op jit(solution)/shard_map/pre_parts/pallas_call | solution.py:147
  18.4 0.0 copy-start.8
  18.4 1.3 broadcast_select_fusion.2
  19.7 0.0 copy-done.8
  19.7 1.5 collective-permute-start.3
  21.2 9.3 %back_parts.3 = (bf16[256,2048]{1,0:T(8,128)(2,1)}, bf16[256,2048]{1,0:T(8,128)(2,1)}, bf16[256,2048]{1,0:T(8,128)(2,1)}, bf16[256,2048]{1,0:T(8,128)(2,1)}) custom-call(s32[5]{0:T(128)S(1)} %stack.23.place, bf16[128,4096]{1,0:T(8,128)(2,1)} %copy-done.11, bf16[128,4096]{1,0:T(8,128)(2,1)} %collective-permute-done.4.refs_1_.refs_4_, bf16[4096,2048]{1,0:T(8,128)(2,1)} %refs_2_.5), custom_call_target="tpu_custom_call" | custom-call | flops 1 | bytes 1 | tf_op jit(solution)/shard_map/back_parts/pallas_call | solution.py:231
  30.5 0.7 collective-permute-done.1.refs_0_.refs_5_
  31.2 3.3 %collective-permute-done.3.refs_1_ = bf16[256,2048]{1,0:T(8,128)(2,1)S(1)} collective-permute-done((bf16[256,2048]{1,0:T(8,128)(2,1)S(1)}, bf16[256,2048]{1,0:T(8,128)(2,1)S(1)}, u32[]{:S(2)}, u32[]{:S(2)}) %collective-permute-start.3) | collective-permute-done | bytes 1048608 | tf_op jit(solution)/shard_map/p2/ppermute | solution.py:384
  34.5 1.5 collective-permute-start.5
  36.0 1.6 collective-permute-start.10
  37.6 1.3 collective-permute-start.9
  38.9 9.4 %pre_parts.4 = (bf16[128,4096]{1,0:T(8,128)(2,1)}, bf16[128,2048]{1,0:T(8,128)(2,1)}, bf16[128,2048]{1,0:T(8,128)(2,1)}, bf16[128,4096]{1,0:T(8,128)(2,1)}, bf16...) custom-call(s32[5]{0:T(128)S(1)} %stack.23.place, ...), custom_call_target="tpu_custom_call", output_to_operand_aliasing={{0}: (5, {}), {1}: (6, {}), {2}: (7, {}), {3}: (8, {}), {4}... | custom-call | flops 1 | bytes 1 | tf_op jit(solution)/shard_map/pre_parts/pallas_call | solution.py:147
  48.3 0.1 collective-permute-start.6
  48.4 0.5 collective-permute-start.7
  48.9 0.7 collective-permute-done.5.refs_2_
  49.5 0.9 collective-permute-done.6.refs_1_.refs_2_
  50.5 0.7 collective-permute-done.7.refs_2_.refs_3_
  51.2 1.2 copy-done.2
  52.5 0.2 add_parts.5
  52.7 6.7 %collective-permute-start.8 = (bf16[128,4096]{1,0:T(8,128)(2,1)S(1)}, bf16[128,4096]{1,0:T(8,128)(2,1)S(1)}, u32[]{:S(2)}, u32[]{:S(2)}) collective-permute-start(bf16[128,4096]{1,0:T(8,128)(2,1)S(1)} %add_parts.5), channel_id=1, source_target_pairs={{0,2},{1,3},{6,4},{7,5},{8,10},{9,11},{14,12},{15,13},{16,18},{17,... | collective-permute-start | bytes 3145736 | tf_op jit(solution)/shard_map/ra1/ppermute | solution.py:379
  59.4 14.4 %pre_parts.5 = (bf16[128,4096]{1,0:T(8,128)(2,1)}, bf16[128,2048]{1,0:T(8,128)(2,1)}, bf16[128,2048]{1,0:T(8,128)(2,1)}, bf16[128,4096]{1,0:T(8,128)(2,1)}, bf16...) custom-call(s32[5]{0:T(128)S(1)} %stack.23.place, ...), custom_call_target="tpu_custom_call", output_to_operand_aliasing={{0}: (6, {}), {1}: (7, {}), {2}: (8, {}), {3}: (9, {}), {4}... | custom-call | flops 1 | bytes 1 | tf_op jit(solution)/shard_map/pre_parts/pallas_call | solution.py:147
  73.9 0.1 collective-permute-start.12
  74.0 0.5 collective-permute-start.13
  74.5 1.4 broadcast_select_fusion.1.refs_2_.refs_7_
  75.8 0.0 copy-start.3
  75.8 0.1 collective-permute-start.19
  76.0 0.1 collective-permute-done.12.refs_1_.refs_2_
  76.1 1.4 collective-permute-start.15
  77.5 0.4 collective-permute-start.16
  77.9 4.1 %collective-permute-done.8.refs_1_ = bf16[128,4096]{1,0:T(8,128)(2,1)S(1)} collective-permute-done((bf16[128,4096]{1,0:T(8,128)(2,1)S(1)}, bf16[128,4096]{1,0:T(8,128)(2,1)S(1)}, u32[]{:S(2)}, u32[]{:S(2)}) %collective-permute-start.8) | collective-permute-done | bytes 1048608 | tf_op jit(solution)/shard_map/ra1/ppermute | solution.py:379
  82.1 0.2 add_parts.7
  82.3 0.4 add_parts.6
  82.7 4.5 %collective-permute-start.14 = (bf16[128,4096]{1,0:T(8,128)(2,1)S(1)}, bf16[128,4096]{1,0:T(8,128)(2,1)S(1)}, u32[]{:S(2)}, u32[]{:S(2)}) collective-permute-start(bf16[128,4096]{1,0:T(8,128)(2,1)S(1)} %add_parts.7), channel_id=1, source_target_pairs={{0,2},{1,3},{6,4},{7,5},{8,10},{9,11},{14,12},{15,13},{16,18},{17,... | collective-permute-start | bytes 3145736 | tf_op jit(solution)/shard_map/ra2/ppermute | solution.py:379
  87.2 0.7 collective-permute-start.11
  88.0 1.0 copy-done.14
  89.0 1.0 copy-done.15
  89.9 14.5 %back_parts.4 = (bf16[256,2048]{1,0:T(8,128)(2,1)}, bf16[256,2048]{1,0:T(8,128)(2,1)}, bf16[256,2048]{1,0:T(8,128)(2,1)}, bf16[256,2048]{1,0:T(8,128)(2,1)}) custom-call(s32[5]{0:T(128)S(1)} %stack.23.place, bf16[128,4096]{1,0:T(8,128)(2,1)} %collective-permute-done.1.refs_0_.refs_5_, ...), custom_call_target="tpu_custom_call", output_to_operand_aliasing={{0}: (6, {}), {1}: (7, {}), {2}: (8, {}), {3}: (9, {})} | custom-call | flops 1 | bytes 1 | tf_op jit(solution)/shard_map/back_parts/pallas_call | solution.py:231
  104.4 0.1 broadcast_select_fusion.refs_0_.refs_9_
  104.6 0.3 collective-permute-start.20
  104.8 5.4 %collective-permute-done.14.refs_1_ = bf16[128,4096]{1,0:T(8,128)(2,1)S(1)} collective-permute-done((bf16[128,4096]{1,0:T(8,128)(2,1)S(1)}, bf16[128,4096]{1,0:T(8,128)(2,1)S(1)}, u32[]{:S(2)}, u32[]{:S(2)}) %collective-permute-start.14) | collective-permute-done | bytes 1048608 | tf_op jit(solution)/shard_map/ra2/ppermute | solution.py:379
  110.2 1.0 copy-done.16
  111.2 9.3 %back_parts.5 = (bf16[256,2048]{1,0:T(8,128)(2,1)}, bf16[256,2048]{1,0:T(8,128)(2,1)}, bf16[256,2048]{1,0:T(8,128)(2,1)}, bf16[256,2048]{1,0:T(8,128)(2,1)}) custom-call(s32[5]{0:T(128)S(1)} %stack.23.place, bf16[128,4096]{1,0:T(8,128)(2,1)} %copy-done.10, ...), custom_call_target="tpu_custom_call", output_to_operand_aliasing={{0}: (4, {}), {1}: (5, {}), {2}: (6, {}), {3}: (7, {})} | custom-call | flops 1 | bytes 1 | tf_op jit(solution)/shard_map/back_parts/pallas_call | solution.py:231
  120.5 0.6 collective-permute-start.21
  121.1 0.4 add_parts.9
  121.5 0.9 collective-permute-start.23
  122.4 0.4 add_parts.8
  122.8 7.1 %collective-permute-start.22 = (bf16[128,4096]{1,0:T(8,128)(2,1)S(1)}, bf16[128,4096]{1,0:T(8,128)(2,1)S(1)}, u32[]{:S(2)}, u32[]{:S(2)}) collective-permute-start(bf16[128,4096]{1,0:T(8,128)(2,1)S(1)} %add_parts.8), channel_id=1, source_target_pairs={{0,2},{1,3},{2,0},{3,1},{4,6},{5,7},{6,4},{7,5},{8,10},{9,11},{10,... | collective-permute-start | bytes 3145736 | tf_op jit(solution)/shard_map/ra3/ppermute | solution.py:379
  129.9 1.5 collective-permute-start.24
  131.4 20.2 %weight_grads.2 = (f32[4096,2048]{1,0:T(8,128)}, f32[1,4096]{1,0:T(1,128)}) custom-call(s32[5]{0:T(128)S(1)} %stack.23.place, bf16[256,2048]{1,0:T(8,128)(2,1)} %own.9, bf16[256,2048]{1,0:T(8,128)(2,1)} %copy-done.8, bf16[256,2048]{1,0:T(8,128)(2,1)} %copy-done.12, bf16[256,2048]{1,0:T(8,128)(2,1)} %copy-done.13, bf16[128,4096]{1,0:T(8,128)(2,1)} %copy-done.11, ...), custom_call_target="tpu_custom_call" | custom-call | flops 1 | bytes 1 | tf_op jit(solution)/shard_map/weight_grads/pallas_call | solution.py:271
  151.6 0.0 copy-start.23
  151.6 0.2 add_pair.1
  151.9 0.5 collective-permute-start.27
  152.4 0.2 copy-done.22
  152.6 0.0 copy-start.4
  152.7 10.6 %weight_grads.3 = (f32[4096,2048]{1,0:T(8,128)}, f32[1,4096]{1,0:T(1,128)}) custom-call(s32[5]{0:T(128)S(1)} %stack.23.place, bf16[256,2048]{1,0:T(8,128)(2,1)} %own.9, bf16[256,2048]{1,0:T(8,128)(2,1)} %copy-done.8, bf16[256,2048]{1,0:T(8,128)(2,1)} %copy-done.12, bf16[256,2048]{1,0:T(8,128)(2,1)} %copy-done.13, ...), custom_call_target="tpu_custom_call", output_to_operand_aliasing={{0}: (13, {}), {1}: (14, {})} | custom-call | flops 1 | bytes 1 | tf_op jit(solution)/shard_map/weight_grads/pallas_call | solution.py:271
  163.3 1.7 %base_grads.1 = bf16[128,4096]{1,0:T(8,128)(2,1)} custom-call(bf16[128,4096]{1,0:T(8,128)(2,1)S(1)} %copy-done.4, bf16[1,4096]{1,0:T(2,128)(2,1)S(1)} %broadcast_in_dim.3.bias, bf16[128,4096]{1,0:T(8,128)(2,1)S(1)} %copy-done.6, bf16[128,2048]{1,0:T(8,128)(2,1)S(1)} %collective-permute-done.25.refs_0_, ...), custom_call_target="tpu_custom_call" | custom-call | flops 1 | bytes 524288 | tf_op jit(solution)/shard_map/base_grads/pallas_call | solution.py:346
  165.0 1.7 %collective-permute-done.27 = bf16[256,2048]{1,0:T(8,128)(2,1)S(1)} collective-permute-done((bf16[256,2048]{1,0:T(8,128)(2,1)S(1)}, bf16[256,2048]{1,0:T(8,128)(2,1)S(1)}, u32[]{:S(2)}, u32[]{:S(2)}) %collective-permute-start.27) | collective-permute-done | bytes 1048608 | tf_op jit(solution)/shard_map/e2/ppermute | solution.py:384
  166.7 1.5 add_convert_fusion
  (62 shorter events, 0.1 us)
Async XLA Ops:
  0.6 17.8 %collective-permute-start = (bf16[256,2048]{1,0:T(8,128)(2,1)}, bf16[256,2048]{1,0:T(8,128)(2,1)S(1)}, u32[]{:S(2)}, u32[]{:S(2)}) collective-permute-start(bf16[256,2048]{1,0:T(8,128)(2,1)} %own.9), channel_id=1, source_target_pairs={{0,8},{8,0},{16,24},{24,16},{1,17},{9,25},{17,1},{25,9},{2,10},{10... | collective-permute-start | bytes 3145736 | tf_op jit(solution)/shard_map/p1/ppermute | solution.py:384
  5.4 13.0 %copy-start.11 = (bf16[128,4096]{1,0:T(8,128)(2,1)}, bf16[128,4096]{1,0:T(8,128)(2,1)S(1)}, u32[]{:S(2)}) copy-start(bf16[128,4096]{1,0:T(8,128)(2,1)S(1)} %multiply_convert_fusion.refs_0_.refs_3_) | copy-start | bytes 3145732
  5.4 15.8 %collective-permute-start.4 = (bf16[128,4096]{1,0:T(8,128)(2,1)S(1)}, bf16[128,4096]{1,0:T(8,128)(2,1)}, u32[]{:S(2)}, u32[]{:S(2)}) collective-permute-start(bf16[128,4096]{1,0:T(8,128)(2,1)S(1)} %multiply_convert_fusion.refs_0_.refs_3_), channel_id=1, source_target_pairs={{0,1},{1,0},{2,3},{3,2},{4,5},{5,4},{6,7},{7,6},{8,9},{9,8},{10,11... | collective-permute-start | bytes 3145736 | tf_op jit(solution)/shard_map/h0/ppermute | solution.py:375
  5.5 25.7 %collective-permute-start.1 = (bf16[128,4096]{1,0:T(8,128)(2,1)S(1)}, bf16[128,4096]{1,0:T(8,128)(2,1)}, u32[]{:S(2)}, u32[]{:S(2)}) collective-permute-start(bf16[128,4096]{1,0:T(8,128)(2,1)S(1)} %multiply_convert_fusion.refs_0_.refs_3_), channel_id=1, source_target_pairs={{0,2},{1,3},{2,0},{3,1},{4,6},{5,7},{6,4},{7,5},{8,10},{9,11},{10,... | collective-permute-start | bytes 3145736 | tf_op jit(solution)/shard_map/a0/ppermute | solution.py:379
  7.2 24.0 %collective-permute-start.2 = (bf16[128,4096]{1,0:T(8,128)(2,1)S(1)}, bf16[128,4096]{1,0:T(8,128)(2,1)}, u32[]{:S(2)}, u32[]{:S(2)}) collective-permute-start(bf16[128,4096]{1,0:T(8,128)(2,1)S(1)} %multiply_convert_fusion.refs_0_.refs_3_), channel_id=1, source_target_pairs={{2,4},{3,5},{4,2},{5,3},{10,12},{11,13},{12,10},{13,11},{18,20},{1... | collective-permute-start | bytes 3145736 | tf_op jit(solution)/shard_map/b0/ppermute | solution.py:379
  8.9 9.5 %copy-start.7 = (bf16[256,2048]{1,0:T(8,128)(2,1)S(1)}, bf16[256,2048]{1,0:T(8,128)(2,1)}, u32[]{:S(2)}) copy-start(bf16[256,2048]{1,0:T(8,128)(2,1)} %own.9) | copy-start | bytes 3145732
  18.4 1.3 copy-start.8
  19.7 14.8 %collective-permute-start.3 = (bf16[256,2048]{1,0:T(8,128)(2,1)S(1)}, bf16[256,2048]{1,0:T(8,128)(2,1)S(1)}, u32[]{:S(2)}, u32[]{:S(2)}) collective-permute-start(bf16[256,2048]{1,0:T(8,128)(2,1)S(1)} %get-tuple-element.157), channel_id=1, source_target_pairs={{0,16},{8,24},{16,0},{24,8},{1,9},{9,1},{17,25},{25,17},{2,18},{10... | collective-permute-start | bytes 3145736 | tf_op jit(solution)/shard_map/p2/ppermute | solution.py:384
  34.5 4.4 %copy-start.12 = (bf16[256,2048]{1,0:T(8,128)(2,1)}, bf16[256,2048]{1,0:T(8,128)(2,1)S(1)}, u32[]{:S(2)}) copy-start(bf16[256,2048]{1,0:T(8,128)(2,1)S(1)} %collective-permute-done.3.refs_1_) | copy-start | bytes 3145732
  34.5 15.0 %collective-permute-start.5 = (bf16[256,2048]{1,0:T(8,128)(2,1)}, bf16[256,2048]{1,0:T(8,128)(2,1)S(1)}, u32[]{:S(2)}, u32[]{:S(2)}) collective-permute-start(bf16[256,2048]{1,0:T(8,128)(2,1)} %get-tuple-element.95), channel_id=1, source_target_pairs={{0,16},{8,24},{16,0},{24,8},{1,9},{9,1},{17,25},{25,17},{2,18},{10... | collective-permute-start | bytes 3145736 | tf_op jit(solution)/shard_map/p3/ppermute | solution.py:384
  36.0 37.9 %collective-permute-start.10 = (bf16[128,4096]{1,0:T(8,128)(2,1)}, bf16[128,4096]{1,0:T(8,128)(2,1)}, u32[]{:S(2)}, u32[]{:S(2)}) collective-permute-start(bf16[128,4096]{1,0:T(8,128)(2,1)} %collective-permute-done.1.refs_0_.refs_5_), channel_id=1, source_target_pairs={{2,4},{3,5},{4,2},{5,3},{10,12},{11,13},{12,10},{13,11},{18,20},{1... | collective-permute-start | bytes 3145736 | tf_op jit(solution)/shard_map/b1/ppermute | solution.py:379
  37.6 36.8 %collective-permute-start.9 = (bf16[128,4096]{1,0:T(8,128)(2,1)}, bf16[128,4096]{1,0:T(8,128)(2,1)}, u32[]{:S(2)}, u32[]{:S(2)}) collective-permute-start(bf16[128,4096]{1,0:T(8,128)(2,1)} %collective-permute-done.2), channel_id=1, source_target_pairs={{2,0},{3,1},{4,6},{5,7},{10,8},{11,9},{12,14},{13,15},{18,16},{19,... | collective-permute-start | bytes 3145736 | tf_op jit(solution)/shard_map/a1/ppermute | solution.py:379
  48.3 2.2 %collective-permute-start.6 = (bf16[128,2048]{1,0:T(8,128)(2,1)}, bf16[128,2048]{1,0:T(8,128)(2,1)S(1)}, u32[]{:S(2)}, u32[]{:S(2)}) collective-permute-start(bf16[128,2048]{1,0:T(8,128)(2,1)} %get-tuple-element.97), channel_id=1, source_target_pairs={{0,1},{1,0},{2,3},{3,2},{4,5},{5,4},{6,7},{7,6},{8,9},{9,8},{10,11... | collective-permute-start | bytes 1572872 | tf_op jit(solution)/shard_map/o0/ppermute | solution.py:375
  48.4 2.9 %collective-permute-start.7 = (bf16[128,2048]{1,0:T(8,128)(2,1)}, bf16[128,2048]{1,0:T(8,128)(2,1)S(1)}, u32[]{:S(2)}, u32[]{:S(2)}) collective-permute-start(bf16[128,2048]{1,0:T(8,128)(2,1)} %get-tuple-element.98), channel_id=1, source_target_pairs={{0,1},{1,0},{2,3},{3,2},{4,5},{5,4},{6,7},{7,6},{8,9},{9,8},{10,11... | collective-permute-start | bytes 1572872 | tf_op jit(solution)/shard_map/o0/ppermute | solution.py:375
  49.5 9.9 %copy-start.13 = (bf16[256,2048]{1,0:T(8,128)(2,1)}, bf16[256,2048]{1,0:T(8,128)(2,1)S(1)}, u32[]{:S(2)}) copy-start(bf16[256,2048]{1,0:T(8,128)(2,1)S(1)} %collective-permute-done.5.refs_2_) | copy-start | bytes 3145732
  49.5 38.4 %collective-permute-start.18 = (bf16[128,4096]{1,0:T(8,128)(2,1)}, bf16[128,4096]{1,0:T(8,128)(2,1)S(1)}, u32[]{:S(2)}, u32[]{:S(2)}) collective-permute-start(bf16[128,4096]{1,0:T(8,128)(2,1)} %collective-permute-done.1.refs_0_.refs_5_), channel_id=1, source_target_pairs={{0,1},{1,0},{2,3},{3,2},{4,5},{5,4},{6,7},{7,6},{8,9},{9,8},{10,11... | collective-permute-start | bytes 3145736 | tf_op jit(solution)/shard_map/h1/ppermute | solution.py:375
  51.2 1.2 copy-start.2
  52.7 29.3 %collective-permute-start.8 = (bf16[128,4096]{1,0:T(8,128)(2,1)S(1)}, bf16[128,4096]{1,0:T(8,128)(2,1)S(1)}, u32[]{:S(2)}, u32[]{:S(2)}) collective-permute-start(bf16[128,4096]{1,0:T(8,128)(2,1)S(1)} %add_parts.5), channel_id=1, source_target_pairs={{0,2},{1,3},{6,4},{7,5},{8,10},{9,11},{14,12},{15,13},{16,18},{17,... | collective-permute-start | bytes 3145736 | tf_op jit(solution)/shard_map/ra1/ppermute | solution.py:379
  73.8 3.6 %copy-start.19 = (bf16[128,2048]{1,0:T(8,128)(2,1)S(1)}, bf16[128,2048]{1,0:T(8,128)(2,1)}, u32[]{:S(2)}) copy-start(bf16[128,2048]{1,0:T(8,128)(2,1)} %get-tuple-element.118) | copy-start | bytes 1572868
  73.8 8.2 %copy-start.20 = (bf16[128,2048]{1,0:T(8,128)(2,1)S(1)}, bf16[128,2048]{1,0:T(8,128)(2,1)}, u32[]{:S(2)}) copy-start(bf16[128,2048]{1,0:T(8,128)(2,1)} %get-tuple-element.119) | copy-start | bytes 1572868
  73.9 8.2 %copy-start = (bf16[128,4096]{1,0:T(8,128)(2,1)S(1)}, bf16[128,4096]{1,0:T(8,128)(2,1)}, u32[]{:S(2)}) copy-start(bf16[128,4096]{1,0:T(8,128)(2,1)} %get-tuple-element.111.refs_0_) | copy-start | bytes 3145732
  73.9 2.2 %collective-permute-start.12 = (bf16[128,2048]{1,0:T(8,128)(2,1)}, bf16[128,2048]{1,0:T(8,128)(2,1)S(1)}, u32[]{:S(2)}, u32[]{:S(2)}) collective-permute-start(bf16[128,2048]{1,0:T(8,128)(2,1)} %get-tuple-element.115), channel_id=1, source_target_pairs={{0,1},{1,0},{2,3},{3,2},{4,5},{5,4},{6,7},{7,6},{8,9},{9,8},{10,11... | collective-permute-start | bytes 1572872 | tf_op jit(solution)/shard_map/o1/ppermute | solution.py:375
  74.0 3.5 %collective-permute-start.13 = (bf16[128,2048]{1,0:T(8,128)(2,1)}, bf16[128,2048]{1,0:T(8,128)(2,1)S(1)}, u32[]{:S(2)}, u32[]{:S(2)}) collective-permute-start(bf16[128,2048]{1,0:T(8,128)(2,1)} %get-tuple-element.116), channel_id=1, source_target_pairs={{0,1},{1,0},{2,3},{3,2},{4,5},{5,4},{6,7},{7,6},{8,9},{9,8},{10,11... | collective-permute-start | bytes 1572872 | tf_op jit(solution)/shard_map/o1/ppermute | solution.py:375
  75.8 6.9 %copy-start.9 = (bf16[128,4096]{1,0:T(8,128)(2,1)}, bf16[128,4096]{1,0:T(8,128)(2,1)S(1)}, u32[]{:S(2)}) copy-start(bf16[128,4096]{1,0:T(8,128)(2,1)S(1)} %broadcast_select_fusion.1.refs_2_.refs_7_) | copy-start | bytes 3145732
  75.8 6.5 %copy-start.3 = (bf16[128,4096]{1,0:T(8,128)(2,1)S(1)}, bf16[128,4096]{1,0:T(8,128)(2,1)}, u32[]{:S(2)}) copy-start(bf16[128,4096]{1,0:T(8,128)(2,1)} %get-tuple-element.113.refs_0_) | copy-start | bytes 3145732
  75.8 12.1 %collective-permute-start.19 = (bf16[128,4096]{1,0:T(8,128)(2,1)S(1)}, bf16[128,4096]{1,0:T(8,128)(2,1)S(1)}, u32[]{:S(2)}, u32[]{:S(2)}) collective-permute-start(bf16[128,4096]{1,0:T(8,128)(2,1)S(1)} %broadcast_select_fusion.1.refs_2_.refs_7_), channel_id=1, source_target_pairs={{0,1},{1,0},{2,3},{3,2},{4,5},{5,4},{6,7},{7,6},{8,9},{9,8},{10,11... | collective-permute-start | bytes 3145736 | tf_op jit(solution)/shard_map/h2/ppermute | solution.py:375
  76.1 28.4 %collective-permute-start.15 = (bf16[128,4096]{1,0:T(8,128)(2,1)}, bf16[128,4096]{1,0:T(8,128)(2,1)S(1)}, u32[]{:S(2)}, u32[]{:S(2)}) collective-permute-start(bf16[128,4096]{1,0:T(8,128)(2,1)} %collective-permute-done.10), channel_id=1, source_target_pairs={{2,0},{3,1},{4,6},{5,7},{10,8},{11,9},{12,14},{13,15},{18,16},{19,... | collective-permute-start | bytes 3145736 | tf_op jit(solution)/shard_map/a2/ppermute | solution.py:379
  77.5 5.2 %collective-permute-start.16 = (bf16[128,2048]{1,0:T(8,128)(2,1)S(1)}, bf16[128,2048]{1,0:T(8,128)(2,1)S(1)}, u32[]{:S(2)}, u32[]{:S(2)}) collective-permute-start(bf16[128,2048]{1,0:T(8,128)(2,1)S(1)} %copy-done.19), channel_id=1, source_target_pairs={{0,1},{1,0},{2,3},{3,2},{4,5},{5,4},{6,7},{7,6},{8,9},{9,8},{10,11... | collective-permute-start | bytes 1572872 | tf_op jit(solution)/shard_map/o2/ppermute | solution.py:375
  82.0 5.2 %collective-permute-start.17 = (bf16[128,2048]{1,0:T(8,128)(2,1)S(1)}, bf16[128,2048]{1,0:T(8,128)(2,1)S(1)}, u32[]{:S(2)}, u32[]{:S(2)}) collective-permute-start(bf16[128,2048]{1,0:T(8,128)(2,1)S(1)} %copy-done.20), channel_id=1, source_target_pairs={{0,1},{1,0},{2,3},{3,2},{4,5},{5,4},{6,7},{7,6},{8,9},{9,8},{10,11... | collective-permute-start | bytes 1572872 | tf_op jit(solution)/shard_map/o2/ppermute | solution.py:375
  82.7 27.5 %collective-permute-start.14 = (bf16[128,4096]{1,0:T(8,128)(2,1)S(1)}, bf16[128,4096]{1,0:T(8,128)(2,1)S(1)}, u32[]{:S(2)}, u32[]{:S(2)}) collective-permute-start(bf16[128,4096]{1,0:T(8,128)(2,1)S(1)} %add_parts.7), channel_id=1, source_target_pairs={{0,2},{1,3},{6,4},{7,5},{8,10},{9,11},{14,12},{15,13},{16,18},{17,... | collective-permute-start | bytes 3145736 | tf_op jit(solution)/shard_map/ra2/ppermute | solution.py:379
  87.2 23.0 %collective-permute-start.11 = (bf16[128,4096]{1,0:T(8,128)(2,1)S(1)}, bf16[128,4096]{1,0:T(8,128)(2,1)S(1)}, u32[]{:S(2)}, u32[]{:S(2)}) collective-permute-start(bf16[128,4096]{1,0:T(8,128)(2,1)S(1)} %add_parts.6), channel_id=1, source_target_pairs={{2,4},{3,5},{4,2},{5,3},{10,12},{11,13},{12,10},{13,11},{18,20},{1... | collective-permute-start | bytes 3145736 | tf_op jit(solution)/shard_map/rb2/ppermute | solution.py:379
  88.0 1.0 copy-start.14
  88.9 1.0 copy-start.15
  104.6 5.7 %copy-start.10 = (bf16[128,4096]{1,0:T(8,128)(2,1)}, bf16[128,4096]{1,0:T(8,128)(2,1)S(1)}, u32[]{:S(2)}) copy-start(bf16[128,4096]{1,0:T(8,128)(2,1)S(1)} %broadcast_select_fusion.refs_0_.refs_9_) | copy-start | bytes 3145732
  104.6 16.5 %copy-start.21 = (bf16[128,2048]{1,0:T(8,128)(2,1)S(1)}, bf16[128,2048]{1,0:T(8,128)(2,1)}, u32[]{:S(2)}) copy-start(bf16[128,2048]{1,0:T(8,128)(2,1)} %get-tuple-element.147) | copy-start | bytes 1572868
  104.6 5.6 %collective-permute-start.20 = (bf16[128,4096]{1,0:T(8,128)(2,1)S(1)}, bf16[128,4096]{1,0:T(8,128)(2,1)S(1)}, u32[]{:S(2)}, u32[]{:S(2)}) collective-permute-start(bf16[128,4096]{1,0:T(8,128)(2,1)S(1)} %broadcast_select_fusion.refs_0_.refs_9_), channel_id=1, source_target_pairs={{0,1},{1,0},{2,3},{3,2},{4,5},{5,4},{6,7},{7,6},{8,9},{9,8},{10,11... | collective-permute-start | bytes 3145736 | tf_op jit(solution)/shard_map/h3/ppermute | solution.py:375
  110.2 1.0 copy-start.16
  120.5 31.1 %collective-permute-start.21 = (bf16[256,2048]{1,0:T(8,128)(2,1)}, bf16[256,2048]{1,0:T(8,128)(2,1)S(1)}, u32[]{:S(2)}, u32[]{:S(2)}) collective-permute-start(bf16[256,2048]{1,0:T(8,128)(2,1)} %get-tuple-element.134), channel_id=1, source_target_pairs={{0,8},{8,0},{16,24},{24,16},{1,17},{9,25},{17,1},{25,9},{2,10},{10... | collective-permute-start | bytes 3145736 | tf_op jit(solution)/shard_map/f1/ppermute | solution.py:384
  121.1 1.3 copy-start.5
  121.1 31.3 %collective-permute-start.25 = (bf16[128,2048]{1,0:T(8,128)(2,1)S(1)}, bf16[128,2048]{1,0:T(8,128)(2,1)S(1)}, u32[]{:S(2)}, u32[]{:S(2)}) collective-permute-start(bf16[128,2048]{1,0:T(8,128)(2,1)S(1)} %copy-done.21), channel_id=1, source_target_pairs={{0,1},{1,0},{2,3},{3,2},{4,5},{5,4},{6,7},{7,6},{8,9},{9,8},{10,11... | collective-permute-start | bytes 1572872 | tf_op jit(solution)/shard_map/o3/ppermute | solution.py:375
  121.5 41.8 %collective-permute-start.23 = (bf16[128,4096]{1,0:T(8,128)(2,1)S(1)}, bf16[128,4096]{1,0:T(8,128)(2,1)S(1)}, u32[]{:S(2)}, u32[]{:S(2)}) collective-permute-start(bf16[128,4096]{1,0:T(8,128)(2,1)S(1)} %add_parts.9), channel_id=1, source_target_pairs={{2,4},{3,5},{4,2},{5,3},{10,12},{11,13},{12,10},{13,11},{18,20},{1... | collective-permute-start | bytes 3145736 | tf_op jit(solution)/shard_map/rb3/ppermute | solution.py:379
  122.4 7.5 %copy-start.18 = (bf16[256,2048]{1,0:T(8,128)(2,1)S(1)}, bf16[256,2048]{1,0:T(8,128)(2,1)}, u32[]{:S(2)}) copy-start(bf16[256,2048]{1,0:T(8,128)(2,1)} %get-tuple-element.146) | copy-start | bytes 3145732
  122.8 40.4 %collective-permute-start.22 = (bf16[128,4096]{1,0:T(8,128)(2,1)S(1)}, bf16[128,4096]{1,0:T(8,128)(2,1)S(1)}, u32[]{:S(2)}, u32[]{:S(2)}) collective-permute-start(bf16[128,4096]{1,0:T(8,128)(2,1)S(1)} %add_parts.8), channel_id=1, source_target_pairs={{0,2},{1,3},{2,0},{3,1},{4,6},{5,7},{6,4},{7,5},{8,10},{9,11},{10,... | collective-permute-start | bytes 3145736 | tf_op jit(solution)/shard_map/ra3/ppermute | solution.py:379
  129.9 21.7 %copy-start.1 = (bf16[256,2048]{1,0:T(8,128)(2,1)S(1)}, bf16[256,2048]{1,0:T(8,128)(2,1)}, u32[]{:S(2)}) copy-start(bf16[256,2048]{1,0:T(8,128)(2,1)} %get-tuple-element.133.a) | copy-start | bytes 3145732
  129.9 33.3 %collective-permute-start.24 = (bf16[256,2048]{1,0:T(8,128)(2,1)S(1)}, bf16[256,2048]{1,0:T(8,128)(2,1)S(1)}, u32[]{:S(2)}, u32[]{:S(2)}) collective-permute-start(bf16[256,2048]{1,0:T(8,128)(2,1)S(1)} %copy-done.18), channel_id=1, source_target_pairs={{0,8},{8,0},{16,24},{24,16},{1,17},{9,25},{17,1},{25,9},{2,10},{10... | collective-permute-start | bytes 3145736 | tf_op jit(solution)/shard_map/e1/ppermute | solution.py:384
  151.6 1.0 copy-start.22
  151.6 1.0 copy-start.23
  151.9 14.9 %collective-permute-start.27 = (bf16[256,2048]{1,0:T(8,128)(2,1)S(1)}, bf16[256,2048]{1,0:T(8,128)(2,1)S(1)}, u32[]{:S(2)}, u32[]{:S(2)}) collective-permute-start(bf16[256,2048]{1,0:T(8,128)(2,1)S(1)} %add_pair.1), channel_id=1, source_target_pairs={{0,16},{8,24},{16,0},{24,8},{1,9},{9,1},{17,25},{25,17},{2,18},{10... | collective-permute-start | bytes 3145736 | tf_op jit(solution)/shard_map/e2/ppermute | solution.py:384
  152.6 10.6 %collective-permute-start.26 = (bf16[128,2048]{1,0:T(8,128)(2,1)S(1)}, bf16[128,2048]{1,0:T(8,128)(2,1)S(1)}, u32[]{:S(2)}, u32[]{:S(2)}) collective-permute-start(bf16[128,2048]{1,0:T(8,128)(2,1)S(1)} %copy-done.22), channel_id=1, source_target_pairs={{0,1},{1,0},{2,3},{3,2},{4,5},{5,4},{6,7},{7,6},{8,9},{9,8},{10,11... | collective-permute-start | bytes 1572872 | tf_op jit(solution)/shard_map/o3/ppermute | solution.py:375
  152.6 10.6 %copy-start.4 = (bf16[128,4096]{1,0:T(8,128)(2,1)S(1)}, bf16[128,4096]{1,0:T(8,128)(2,1)}, u32[]{:S(2)}) copy-start(bf16[128,4096]{1,0:T(8,128)(2,1)} %grad.1) | copy-start | bytes 3145732
  152.6 10.6 %copy-start.6 = (bf16[128,4096]{1,0:T(8,128)(2,1)S(1)}, bf16[128,4096]{1,0:T(8,128)(2,1)}, u32[]{:S(2)}) copy-start(bf16[128,4096]{1,0:T(8,128)(2,1)} %get-tuple-element.145.q) | copy-start | bytes 3145732
  163.3 3.4 %copy-start.17 = (bf16[256,2048]{1,0:T(8,128)(2,1)S(1)}, bf16[256,2048]{1,0:T(8,128)(2,1)}, u32[]{:S(2)}) copy-start(bf16[256,2048]{1,0:T(8,128)(2,1)} %get-tuple-element.153) | copy-start | bytes 3145732

commit v3 on v2

--- a/solution.py
+++ b/solution.py
@@ -245,7 +245,7 @@
         compiler_params=params(28),
         cost_estimate=cost(2 * n_h * lanes * depth * wide, 2 * wide * depth),
         name="back_parts",
-    )(place, *in_hbm(*hs, w, *prior))
+    )(place, *hs, *in_hbm(w, *prior))
 
 
 def weight_kernel(n_h, n_prior, place, own, *refs):
@@ -451,7 +451,7 @@
     hs = (own_h, h0, a0, h1, s2, h2, s3, h3)
     tile = 512
     tiles = base_input.shape[1] // tile
-    early = tiles * 3 // 4
+    early = tiles * 5 // 8
     got = (p1, p2, p3)
     grads = weight_grads(after(place, to_ra3, to_rb3), layer_input, got, hs, tile, 0, early)
     to_e2 = add_pair(relayed, after(f1, *grads))

time: 169 us -> 168 us (level)
  local copies, waits for them, and re-layouts: 4.59 us -> 1.61 us
    unnamed x48, local copies, waits for them, and re-layouts: 4.49 us -> 1.52 us
    ppermute x10, waiting for transfers between devices: 10.1 us -> 12.4 us  [line(): return lax.ppermute(a, 'col', line_pairs(hops))]
  transfers between devices with their start and end apart: 28 -> 28, of which waited for: 9 -> 8; matrix products, arithmetic and copies ran while one was open for 3% -> 4% of each run, Pallas kernels for 54% -> 54%
where the time goes in v3:
time: 168 us
  Pallas kernels  99.6 us (59%)
  starting transfers between devices  38.6 us (23%)
  waiting for transfers between devices  19.1 us (11%)
  other arithmetic  7.49 us (4%)
    pallas_call x3, Pallas kernels, pre_parts(): pl.pallas_call(functools.partial(pre_kernel, turns, slots, len(got), len(...  33.5 us
    pallas_call x3, Pallas kernels, back_parts(): pl.pallas_call(functools.partial(back_kernel, tuple(slots), by_role, len(...  31.7 us
    pallas_call x2, Pallas kernels, weight_grads(): pl.pallas_call(functools.partial(weight_kernel, n_h, len(prior)), grid=(c...  30.8 us
    ppermute x10, starting transfers between devices, line(): return lax.ppermute(a, 'col', line_pairs(hops))  28.2 us
    ppermute x10, waiting for transfers between devices, line(): return lax.ppermute(a, 'col', line_pairs(hops))  12.4 us
    ppermute x6, starting transfers between devices, plane(): return lax.ppermute(a, ('row', 'col'), pairs)  8.54 us
    ppermute x6, waiting for transfers between devices, plane(): return lax.ppermute(a, ('row', 'col'), pairs)  4.79 us
  transfers between devices with their start and end apart: 28, of which 8 were waited for; matrix products, arithmetic and copies ran while one was open for 4% of the time, Pallas kernels for 54%

profile of v3, /device:TPU:0, one launch (start us, length us, event | category | flops | bytes accessed | tf_op | source)
XLA Modules:
  0.0 167.6 jit_solution(4886830972073122243)
XLA Ops:
  0.6 3.0 %collective-permute-start = (bf16[256,2048]{1,0:T(8,128)(2,1)}, bf16[256,2048]{1,0:T(8,128)(2,1)}, u32[]{:S(2)}, u32[]{:S(2)}) collective-permute-start(bf16[256,2048]{1,0:T(8,128)(2,1)} %own.9), channel_id=1, source_target_pairs={{0,8},{8,0},{16,24},{24,16},{1,17},{9,25},{17,1},{25,9},{2,10},{10... | collective-permute-start | bytes 3145736 | tf_op jit(solution)/shard_map/p1/ppermute | solution.py:384
  3.6 1.8 %multiply_convert_fusion.refs_0_.refs_3_ = bf16[128,4096]{1,0:T(8,128)(2,1)S(1)} fusion(bf16[128,4096]{1,0:T(8,128)(2,1)} %param.5, bf16[128,4096]{1,0:T(8,128)(2,1)} %grad.1), kind=kLoop, calls=%fused_computation.1 | loop fusion | flops 2097152 | bytes 3145728 | tf_op jit(solution)/shard_map/convert_element_type | solution.py:407
  5.4 0.1 collective-permute-start.4
  5.5 1.6 collective-permute-start.1
  7.2 1.7 collective-permute-start.2
  8.8 0.1 stack.23.place
  8.9 9.6 %pre_parts.3 = (bf16[128,4096]{1,0:T(8,128)(2,1)}, bf16[128,2048]{1,0:T(8,128)(2,1)}, bf16[128,2048]{1,0:T(8,128)(2,1)}, bf16[128,4096]{1,0:T(8,128)(2,1)}, bf16...) custom-call(s32[5]{0:T(128)S(1)} %stack.23.place, ...), custom_call_target="tpu_custom_call" | custom-call | flops 1 | bytes 1 | tf_op jit(solution)/shard_map/pre_parts/pallas_call | solution.py:147
  18.5 0.0 collective-permute-done.refs_0_
  18.5 2.7 %broadcast_select_fusion.2 = (bf16[256,2048]{1,0:T(8,128)(2,1)}, bf16[256,2048]{1,0:T(8,128)(2,1)S(1)}) fusion(bf16[256,2048]{1,0:T(8,128)(2,1)} %own.9, bf16[256,2048]{1,0:T(8,128)(2,1)} %collective-permute-done.refs_0_, pred[]{:T(512)S(6)} %eq.23), kind=kLoop, calls=%fused_computation.4 | loop fusion | flops 1048576 | bytes 4194305 | tf_op jit(solution)/shard_map/jit(_where)/select_n | solution.py:414
  21.2 1.5 collective-permute-start.3
  22.6 9.1 %back_parts.3 = (bf16[256,2048]{1,0:T(8,128)(2,1)}, bf16[256,2048]{1,0:T(8,128)(2,1)}, bf16[256,2048]{1,0:T(8,128)(2,1)}, bf16[256,2048]{1,0:T(8,128)(2,1)}) custom-call(s32[5]{0:T(128)S(1)} %stack.23.place, bf16[128,4096]{1,0:T(8,128)(2,1)S(1)} %multiply_convert_fusion.refs_0_.refs_3_, bf16[128,4096]{1,0:T(8,128)(2,1)S(1)} %collective-permute-done.4.refs_1_.refs_4_, ...), custom_call_target="tpu_custom_call" | custom-call | flops 1 | bytes 1 | tf_op jit(solution)/shard_map/back_parts/pallas_call | solution.py:231
  31.7 0.0 collective-permute-done.2
  31.8 4.2 %collective-permute-done.3.refs_1_ = bf16[256,2048]{1,0:T(8,128)(2,1)S(1)} collective-permute-done((bf16[256,2048]{1,0:T(8,128)(2,1)S(1)}, bf16[256,2048]{1,0:T(8,128)(2,1)S(1)}, u32[]{:S(2)}, u32[]{:S(2)}) %collective-permute-start.3) | collective-permute-done | bytes 1048608 | tf_op jit(solution)/shard_map/p2/ppermute | solution.py:384
  36.0 1.5 collective-permute-start.5
  37.4 1.6 collective-permute-start.10
  39.1 1.3 collective-permute-start.9
  40.4 9.5 %pre_parts.4 = (bf16[128,4096]{1,0:T(8,128)(2,1)}, bf16[128,2048]{1,0:T(8,128)(2,1)}, bf16[128,2048]{1,0:T(8,128)(2,1)}, bf16[128,4096]{1,0:T(8,128)(2,1)}, bf16...) custom-call(s32[5]{0:T(128)S(1)} %stack.23.place, ...), custom_call_target="tpu_custom_call", output_to_operand_aliasing={{0}: (5, {}), {1}: (6, {}), {2}: (7, {}), {3}: (8, {}), {4}... | custom-call | flops 1 | bytes 1 | tf_op jit(solution)/shard_map/pre_parts/pallas_call | solution.py:147
  49.8 0.1 collective-permute-start.6
  49.9 0.5 collective-permute-start.7
  50.4 0.6 collective-permute-done.5.refs_2_
  51.0 0.0 collective-permute-start.18
  51.0 1.0 collective-permute-done.6.refs_1_.refs_2_
  52.0 0.7 collective-permute-done.7.refs_2_.refs_3_
  52.8 1.2 copy-done.10
  54.0 0.2 add_parts.5
  54.2 7.4 %collective-permute-start.8 = (bf16[128,4096]{1,0:T(8,128)(2,1)S(1)}, bf16[128,4096]{1,0:T(8,128)(2,1)S(1)}, u32[]{:S(2)}, u32[]{:S(2)}) collective-permute-start(bf16[128,4096]{1,0:T(8,128)(2,1)S(1)} %add_parts.5), channel_id=1, source_target_pairs={{0,2},{1,3},{6,4},{7,5},{8,10},{9,11},{14,12},{15,13},{16,18},{17,... | collective-permute-start | bytes 3145736 | tf_op jit(solution)/shard_map/ra1/ppermute | solution.py:379
  61.7 14.5 %pre_parts.5 = (bf16[128,4096]{1,0:T(8,128)(2,1)}, bf16[128,2048]{1,0:T(8,128)(2,1)}, bf16[128,2048]{1,0:T(8,128)(2,1)}, bf16[128,4096]{1,0:T(8,128)(2,1)}, bf16...) custom-call(s32[5]{0:T(128)S(1)} %stack.23.place, ...), custom_call_target="tpu_custom_call", output_to_operand_aliasing={{0}: (6, {}), {1}: (7, {}), {2}: (8, {}), {3}: (9, {}), {4}... | custom-call | flops 1 | bytes 1 | tf_op jit(solution)/shard_map/pre_parts/pallas_call | solution.py:147
  76.2 0.1 collective-permute-start.12
  76.3 0.0 collective-permute-done.10
  76.3 0.5 collective-permute-start.13
  76.8 0.0 collective-permute-done.9
  76.8 1.4 broadcast_select_fusion.1.refs_2_.refs_7_
  78.1 0.0 copy-start.11
  78.2 0.1 collective-permute-start.19
  78.3 0.1 collective-permute-done.12.refs_1_.refs_2_
  78.4 1.4 collective-permute-start.15
  79.8 0.0 collective-permute-done.13.refs_2_.refs_3_
  79.8 0.4 collective-permute-start.16
  80.2 4.1 %collective-permute-done.8.refs_1_ = bf16[128,4096]{1,0:T(8,128)(2,1)S(1)} collective-permute-done((bf16[128,4096]{1,0:T(8,128)(2,1)S(1)}, bf16[128,4096]{1,0:T(8,128)(2,1)S(1)}, u32[]{:S(2)}, u32[]{:S(2)}) %collective-permute-start.8) | collective-permute-done | bytes 1048608 | tf_op jit(solution)/shard_map/ra1/ppermute | solution.py:379
  84.3 0.2 add_parts.7
  84.6 0.4 add_parts.6
  85.0 4.5 %collective-permute-start.14 = (bf16[128,4096]{1,0:T(8,128)(2,1)S(1)}, bf16[128,4096]{1,0:T(8,128)(2,1)S(1)}, u32[]{:S(2)}, u32[]{:S(2)}) collective-permute-start(bf16[128,4096]{1,0:T(8,128)(2,1)S(1)} %add_parts.7), channel_id=1, source_target_pairs={{0,2},{1,3},{6,4},{7,5},{8,10},{9,11},{14,12},{15,13},{16,18},{17,... | collective-permute-start | bytes 3145736 | tf_op jit(solution)/shard_map/ra2/ppermute | solution.py:379
  89.4 0.7 collective-permute-start.11
  90.2 13.6 %back_parts.4 = (bf16[256,2048]{1,0:T(8,128)(2,1)}, bf16[256,2048]{1,0:T(8,128)(2,1)}, bf16[256,2048]{1,0:T(8,128)(2,1)}, bf16[256,2048]{1,0:T(8,128)(2,1)}) custom-call(s32[5]{0:T(128)S(1)} %stack.23.place, bf16[128,4096]{1,0:T(8,128)(2,1)S(1)} %collective-permute-done.1.refs_0_.refs_5_, ...), custom_call_target="tpu_custom_call", output_to_operand_aliasing={{0}: (6, {}), {1}: (7, {}), {2}: (8, {}), {3}: (9, {})} | custom-call | flops 1 | bytes 1 | tf_op jit(solution)/shard_map/back_parts/pallas_call | solution.py:231
  103.9 2.2 %collective-permute-done.15 = bf16[128,4096]{1,0:T(8,128)(2,1)S(1)} collective-permute-done((bf16[128,4096]{1,0:T(8,128)(2,1)}, bf16[128,4096]{1,0:T(8,128)(2,1)S(1)}, u32[]{:S(2)}, u32[]{:S(2)}) %collective-permute-start.15) | collective-permute-done | bytes 1048608 | tf_op jit(solution)/shard_map/a2/ppermute | solution.py:379
  106.0 0.1 broadcast_select_fusion.refs_0_.refs_9_
  106.2 0.1 collective-permute-start.20
  106.3 6.2 %collective-permute-done.14.refs_1_ = bf16[128,4096]{1,0:T(8,128)(2,1)S(1)} collective-permute-done((bf16[128,4096]{1,0:T(8,128)(2,1)S(1)}, bf16[128,4096]{1,0:T(8,128)(2,1)S(1)}, u32[]{:S(2)}, u32[]{:S(2)}) %collective-permute-start.14) | collective-permute-done | bytes 1048608 | tf_op jit(solution)/shard_map/ra2/ppermute | solution.py:379
  112.4 9.0 %back_parts.5 = (bf16[256,2048]{1,0:T(8,128)(2,1)}, bf16[256,2048]{1,0:T(8,128)(2,1)}, bf16[256,2048]{1,0:T(8,128)(2,1)}, bf16[256,2048]{1,0:T(8,128)(2,1)}) custom-call(s32[5]{0:T(128)S(1)} %stack.23.place, bf16[128,4096]{1,0:T(8,128)(2,1)S(1)} %broadcast_select_fusion.refs_0_.refs_9_, ...), custom_call_target="tpu_custom_call", output_to_operand_aliasing={{0}: (4, {}), {1}: (5, {}), {2}: (6, {}), {3}: (7, {})} | custom-call | flops 1 | bytes 1 | tf_op jit(solution)/shard_map/back_parts/pallas_call | solution.py:231
  121.5 0.6 collective-permute-start.21
  122.1 0.4 add_parts.9
  122.5 0.9 collective-permute-start.23
  123.4 0.4 add_parts.8
  123.8 7.1 %collective-permute-start.22 = (bf16[128,4096]{1,0:T(8,128)(2,1)S(1)}, bf16[128,4096]{1,0:T(8,128)(2,1)S(1)}, u32[]{:S(2)}, u32[]{:S(2)}) collective-permute-start(bf16[128,4096]{1,0:T(8,128)(2,1)S(1)} %add_parts.8), channel_id=1, source_target_pairs={{0,2},{1,3},{2,0},{3,1},{4,6},{5,7},{6,4},{7,5},{8,10},{9,11},{10,... | collective-permute-start | bytes 3145736 | tf_op jit(solution)/shard_map/ra3/ppermute | solution.py:379
  130.9 1.5 collective-permute-start.24
  132.4 17.8 %weight_grads.2 = (f32[4096,2048]{1,0:T(8,128)}, f32[1,4096]{1,0:T(1,128)}) custom-call(s32[5]{0:T(128)S(1)} %stack.23.place, bf16[256,2048]{1,0:T(8,128)(2,1)} %own.9, bf16[256,2048]{1,0:T(8,128)(2,1)} %collective-permute-done.refs_0_, bf16[256,2048]{1,0:T(8,128)(2,1)} %copy-done.15, bf16[256,2048]{1,0:T(8,128)(2,1)} %copy-done.16, ...), custom_call_target="tpu_custom_call" | custom-call | flops 1 | bytes 1 | tf_op jit(solution)/shard_map/weight_grads/pallas_call | solution.py:271
  150.2 0.0 copy-start.23
  150.2 0.2 add_pair.1
  150.4 0.6 collective-permute-start.27
  151.0 0.2 copy-done.22
  151.2 0.0 copy-start.12
  151.2 13.1 %weight_grads.3 = (f32[4096,2048]{1,0:T(8,128)}, f32[1,4096]{1,0:T(1,128)}) custom-call(s32[5]{0:T(128)S(1)} %stack.23.place, bf16[256,2048]{1,0:T(8,128)(2,1)} %own.9, bf16[256,2048]{1,0:T(8,128)(2,1)} %collective-permute-done.refs_0_, bf16[256,2048]{1,0:T(8,128)(2,1)} %copy-done.15, ...), custom_call_target="tpu_custom_call", output_to_operand_aliasing={{0}: (13, {}), {1}: (14, {})} | custom-call | flops 1 | bytes 1 | tf_op jit(solution)/shard_map/weight_grads/pallas_call | solution.py:271
  164.4 1.7 %base_grads.1 = bf16[128,4096]{1,0:T(8,128)(2,1)} custom-call(bf16[128,4096]{1,0:T(8,128)(2,1)S(1)} %copy-done.12, bf16[1,4096]{1,0:T(2,128)(2,1)S(1)} %broadcast_in_dim.3.bias, bf16[128,4096]{1,0:T(8,128)(2,1)S(1)} %copy-done.14, bf16[128,2048]{1,0:T(8,128)(2,1)S(1)} %collective-permute-done.25.refs_0_, ...), custom_call_target="tpu_custom_call" | custom-call | flops 1 | bytes 524288 | tf_op jit(solution)/shard_map/base_grads/pallas_call | solution.py:346
  166.1 1.6 add_convert_fusion
  (62 shorter events, 0.1 us)
Async XLA Ops:
  0.6 17.9 %collective-permute-start = (bf16[256,2048]{1,0:T(8,128)(2,1)}, bf16[256,2048]{1,0:T(8,128)(2,1)}, u32[]{:S(2)}, u32[]{:S(2)}) collective-permute-start(bf16[256,2048]{1,0:T(8,128)(2,1)} %own.9), channel_id=1, source_target_pairs={{0,8},{8,0},{16,24},{24,16},{1,17},{9,25},{17,1},{25,9},{2,10},{10... | collective-permute-start | bytes 3145736 | tf_op jit(solution)/shard_map/p1/ppermute | solution.py:384
  5.4 17.2 %copy-start.2 = (bf16[128,4096]{1,0:T(8,128)(2,1)}, bf16[128,4096]{1,0:T(8,128)(2,1)S(1)}, u32[]{:S(2)}) copy-start(bf16[128,4096]{1,0:T(8,128)(2,1)S(1)} %multiply_convert_fusion.refs_0_.refs_3_) | copy-start | bytes 3145732
  5.4 17.2 %collective-permute-start.4 = (bf16[128,4096]{1,0:T(8,128)(2,1)S(1)}, bf16[128,4096]{1,0:T(8,128)(2,1)S(1)}, u32[]{:S(2)}, u32[]{:S(2)}) collective-permute-start(bf16[128,4096]{1,0:T(8,128)(2,1)S(1)} %multiply_convert_fusion.refs_0_.refs_3_), channel_id=1, source_target_pairs={{0,1},{1,0},{2,3},{3,2},{4,5},{5,4},{6,7},{7,6},{8,9},{9,8},{10,11... | collective-permute-start | bytes 3145736 | tf_op jit(solution)/shard_map/h0/ppermute | solution.py:375
  5.5 26.2 %collective-permute-start.1 = (bf16[128,4096]{1,0:T(8,128)(2,1)S(1)}, bf16[128,4096]{1,0:T(8,128)(2,1)S(1)}, u32[]{:S(2)}, u32[]{:S(2)}) collective-permute-start(bf16[128,4096]{1,0:T(8,128)(2,1)S(1)} %multiply_convert_fusion.refs_0_.refs_3_), channel_id=1, source_target_pairs={{0,2},{1,3},{2,0},{3,1},{4,6},{5,7},{6,4},{7,5},{8,10},{9,11},{10,... | collective-permute-start | bytes 3145736 | tf_op jit(solution)/shard_map/a0/ppermute | solution.py:379
  7.2 24.6 %collective-permute-start.2 = (bf16[128,4096]{1,0:T(8,128)(2,1)S(1)}, bf16[128,4096]{1,0:T(8,128)(2,1)}, u32[]{:S(2)}, u32[]{:S(2)}) collective-permute-start(bf16[128,4096]{1,0:T(8,128)(2,1)S(1)} %multiply_convert_fusion.refs_0_.refs_3_), channel_id=1, source_target_pairs={{2,4},{3,5},{4,2},{5,3},{10,12},{11,13},{12,10},{13,11},{18,20},{1... | collective-permute-start | bytes 3145736 | tf_op jit(solution)/shard_map/b0/ppermute | solution.py:379
  21.2 14.8 %collective-permute-start.3 = (bf16[256,2048]{1,0:T(8,128)(2,1)S(1)}, bf16[256,2048]{1,0:T(8,128)(2,1)S(1)}, u32[]{:S(2)}, u32[]{:S(2)}) collective-permute-start(bf16[256,2048]{1,0:T(8,128)(2,1)S(1)} %get-tuple-element.157), channel_id=1, source_target_pairs={{0,16},{8,24},{16,0},{24,8},{1,9},{9,1},{17,25},{25,17},{2,18},{10... | collective-permute-start | bytes 3145736 | tf_op jit(solution)/shard_map/p2/ppermute | solution.py:384
  22.6 9.1 %copy-start.9 = (bf16[128,4096]{1,0:T(8,128)(2,1)}, bf16[128,4096]{1,0:T(8,128)(2,1)S(1)}, u32[]{:S(2)}) copy-start(bf16[128,4096]{1,0:T(8,128)(2,1)S(1)} %collective-permute-done.4.refs_1_.refs_4_) | copy-start | bytes 3145732
  31.7 58.5 %copy-start.4 = (bf16[128,4096]{1,0:T(8,128)(2,1)}, bf16[128,4096]{1,0:T(8,128)(2,1)S(1)}, u32[]{:S(2)}) copy-start(bf16[128,4096]{1,0:T(8,128)(2,1)S(1)} %collective-permute-done.1.refs_0_.refs_5_) | copy-start | bytes 3145732
  36.0 4.4 %copy-start.15 = (bf16[256,2048]{1,0:T(8,128)(2,1)}, bf16[256,2048]{1,0:T(8,128)(2,1)S(1)}, u32[]{:S(2)}) copy-start(bf16[256,2048]{1,0:T(8,128)(2,1)S(1)} %collective-permute-done.3.refs_1_) | copy-start | bytes 3145732
  36.0 15.0 %collective-permute-start.5 = (bf16[256,2048]{1,0:T(8,128)(2,1)}, bf16[256,2048]{1,0:T(8,128)(2,1)S(1)}, u32[]{:S(2)}, u32[]{:S(2)}) collective-permute-start(bf16[256,2048]{1,0:T(8,128)(2,1)} %get-tuple-element.95), channel_id=1, source_target_pairs={{0,16},{8,24},{16,0},{24,8},{1,9},{9,1},{17,25},{25,17},{2,18},{10... | collective-permute-start | bytes 3145736 | tf_op jit(solution)/shard_map/p3/ppermute | solution.py:384
  37.4 38.8 %collective-permute-start.10 = (bf16[128,4096]{1,0:T(8,128)(2,1)S(1)}, bf16[128,4096]{1,0:T(8,128)(2,1)}, u32[]{:S(2)}, u32[]{:S(2)}) collective-permute-start(bf16[128,4096]{1,0:T(8,128)(2,1)S(1)} %collective-permute-done.1.refs_0_.refs_5_), channel_id=1, source_target_pairs={{2,4},{3,5},{4,2},{5,3},{10,12},{11,13},{12,10},{13,11},{18,20},{1... | collective-permute-start | bytes 3145736 | tf_op jit(solution)/shard_map/b1/ppermute | solution.py:379
  39.1 37.7 %collective-permute-start.9 = (bf16[128,4096]{1,0:T(8,128)(2,1)}, bf16[128,4096]{1,0:T(8,128)(2,1)}, u32[]{:S(2)}, u32[]{:S(2)}) collective-permute-start(bf16[128,4096]{1,0:T(8,128)(2,1)} %collective-permute-done.2), channel_id=1, source_target_pairs={{2,0},{3,1},{4,6},{5,7},{10,8},{11,9},{12,14},{13,15},{18,16},{19,... | collective-permute-start | bytes 3145736 | tf_op jit(solution)/shard_map/a1/ppermute | solution.py:379
  49.8 2.2 %collective-permute-start.6 = (bf16[128,2048]{1,0:T(8,128)(2,1)}, bf16[128,2048]{1,0:T(8,128)(2,1)S(1)}, u32[]{:S(2)}, u32[]{:S(2)}) collective-permute-start(bf16[128,2048]{1,0:T(8,128)(2,1)} %get-tuple-element.97), channel_id=1, source_target_pairs={{0,1},{1,0},{2,3},{3,2},{4,5},{5,4},{6,7},{7,6},{8,9},{9,8},{10,11... | collective-permute-start | bytes 1572872 | tf_op jit(solution)/shard_map/o0/ppermute | solution.py:375
  49.9 2.9 %collective-permute-start.7 = (bf16[128,2048]{1,0:T(8,128)(2,1)}, bf16[128,2048]{1,0:T(8,128)(2,1)S(1)}, u32[]{:S(2)}, u32[]{:S(2)}) collective-permute-start(bf16[128,2048]{1,0:T(8,128)(2,1)} %get-tuple-element.98), channel_id=1, source_target_pairs={{0,1},{1,0},{2,3},{3,2},{4,5},{5,4},{6,7},{7,6},{8,9},{9,8},{10,11... | collective-permute-start | bytes 1572872 | tf_op jit(solution)/shard_map/o0/ppermute | solution.py:375
  51.0 10.7 %copy-start.16 = (bf16[256,2048]{1,0:T(8,128)(2,1)}, bf16[256,2048]{1,0:T(8,128)(2,1)S(1)}, u32[]{:S(2)}) copy-start(bf16[256,2048]{1,0:T(8,128)(2,1)S(1)} %collective-permute-done.5.refs_2_) | copy-start | bytes 3145732
  51.0 39.2 %collective-permute-start.18 = (bf16[128,4096]{1,0:T(8,128)(2,1)S(1)}, bf16[128,4096]{1,0:T(8,128)(2,1)S(1)}, u32[]{:S(2)}, u32[]{:S(2)}) collective-permute-start(bf16[128,4096]{1,0:T(8,128)(2,1)S(1)} %collective-permute-done.1.refs_0_.refs_5_), channel_id=1, source_target_pairs={{0,1},{1,0},{2,3},{3,2},{4,5},{5,4},{6,7},{7,6},{8,9},{9,8},{10,11... | collective-permute-start | bytes 3145736 | tf_op jit(solution)/shard_map/h1/ppermute | solution.py:375
  52.8 1.2 copy-start.10
  54.2 30.1 %collective-permute-start.8 = (bf16[128,4096]{1,0:T(8,128)(2,1)S(1)}, bf16[128,4096]{1,0:T(8,128)(2,1)S(1)}, u32[]{:S(2)}, u32[]{:S(2)}) collective-permute-start(bf16[128,4096]{1,0:T(8,128)(2,1)S(1)} %add_parts.5), channel_id=1, source_target_pairs={{0,2},{1,3},{6,4},{7,5},{8,10},{9,11},{14,12},{15,13},{16,18},{17,... | collective-permute-start | bytes 3145736 | tf_op jit(solution)/shard_map/ra1/ppermute | solution.py:379
  76.2 3.6 %copy-start.19 = (bf16[128,2048]{1,0:T(8,128)(2,1)S(1)}, bf16[128,2048]{1,0:T(8,128)(2,1)}, u32[]{:S(2)}) copy-start(bf16[128,2048]{1,0:T(8,128)(2,1)} %get-tuple-element.118) | copy-start | bytes 1572868
  76.2 8.2 %copy-start.20 = (bf16[128,2048]{1,0:T(8,128)(2,1)S(1)}, bf16[128,2048]{1,0:T(8,128)(2,1)}, u32[]{:S(2)}) copy-start(bf16[128,2048]{1,0:T(8,128)(2,1)} %get-tuple-element.119) | copy-start | bytes 1572868
  76.2 8.2 %copy-start.3 = (bf16[128,4096]{1,0:T(8,128)(2,1)S(1)}, bf16[128,4096]{1,0:T(8,128)(2,1)}, u32[]{:S(2)}) copy-start(bf16[128,4096]{1,0:T(8,128)(2,1)} %get-tuple-element.111.refs_0_) | copy-start | bytes 3145732
  76.2 2.2 %collective-permute-start.12 = (bf16[128,2048]{1,0:T(8,128)(2,1)}, bf16[128,2048]{1,0:T(8,128)(2,1)S(1)}, u32[]{:S(2)}, u32[]{:S(2)}) collective-permute-start(bf16[128,2048]{1,0:T(8,128)(2,1)} %get-tuple-element.115), channel_id=1, source_target_pairs={{0,1},{1,0},{2,3},{3,2},{4,5},{5,4},{6,7},{7,6},{8,9},{9,8},{10,11... | collective-permute-start | bytes 1572872 | tf_op jit(solution)/shard_map/o1/ppermute | solution.py:375
  76.3 3.5 %collective-permute-start.13 = (bf16[128,2048]{1,0:T(8,128)(2,1)}, bf16[128,2048]{1,0:T(8,128)(2,1)S(1)}, u32[]{:S(2)}, u32[]{:S(2)}) collective-permute-start(bf16[128,2048]{1,0:T(8,128)(2,1)} %get-tuple-element.116), channel_id=1, source_target_pairs={{0,1},{1,0},{2,3},{3,2},{4,5},{5,4},{6,7},{7,6},{8,9},{9,8},{10,11... | collective-permute-start | bytes 1572872 | tf_op jit(solution)/shard_map/o1/ppermute | solution.py:375
  78.1 12.1 %copy-start = (bf16[128,4096]{1,0:T(8,128)(2,1)}, bf16[128,4096]{1,0:T(8,128)(2,1)S(1)}, u32[]{:S(2)}) copy-start(bf16[128,4096]{1,0:T(8,128)(2,1)S(1)} %broadcast_select_fusion.1.refs_2_.refs_7_) | copy-start | bytes 3145732
  78.1 6.4 %copy-start.11 = (bf16[128,4096]{1,0:T(8,128)(2,1)S(1)}, bf16[128,4096]{1,0:T(8,128)(2,1)}, u32[]{:S(2)}) copy-start(bf16[128,4096]{1,0:T(8,128)(2,1)} %get-tuple-element.113.refs_0_) | copy-start | bytes 3145732
  78.2 12.0 %collective-permute-start.19 = (bf16[128,4096]{1,0:T(8,128)(2,1)S(1)}, bf16[128,4096]{1,0:T(8,128)(2,1)S(1)}, u32[]{:S(2)}, u32[]{:S(2)}) collective-permute-start(bf16[128,4096]{1,0:T(8,128)(2,1)S(1)} %broadcast_select_fusion.1.refs_2_.refs_7_), channel_id=1, source_target_pairs={{0,1},{1,0},{2,3},{3,2},{4,5},{5,4},{6,7},{7,6},{8,9},{9,8},{10,11... | collective-permute-start | bytes 3145736 | tf_op jit(solution)/shard_map/h2/ppermute | solution.py:375
  78.4 27.7 %collective-permute-start.15 = (bf16[128,4096]{1,0:T(8,128)(2,1)}, bf16[128,4096]{1,0:T(8,128)(2,1)S(1)}, u32[]{:S(2)}, u32[]{:S(2)}) collective-permute-start(bf16[128,4096]{1,0:T(8,128)(2,1)} %collective-permute-done.10), channel_id=1, source_target_pairs={{2,0},{3,1},{4,6},{5,7},{10,8},{11,9},{12,14},{13,15},{18,16},{19,... | collective-permute-start | bytes 3145736 | tf_op jit(solution)/shard_map/a2/ppermute | solution.py:379
  79.8 5.2 %collective-permute-start.16 = (bf16[128,2048]{1,0:T(8,128)(2,1)S(1)}, bf16[128,2048]{1,0:T(8,128)(2,1)S(1)}, u32[]{:S(2)}, u32[]{:S(2)}) collective-permute-start(bf16[128,2048]{1,0:T(8,128)(2,1)S(1)} %copy-done.19), channel_id=1, source_target_pairs={{0,1},{1,0},{2,3},{3,2},{4,5},{5,4},{6,7},{7,6},{8,9},{9,8},{10,11... | collective-permute-start | bytes 1572872 | tf_op jit(solution)/shard_map/o2/ppermute | solution.py:375
  84.3 5.1 %collective-permute-start.17 = (bf16[128,2048]{1,0:T(8,128)(2,1)S(1)}, bf16[128,2048]{1,0:T(8,128)(2,1)S(1)}, u32[]{:S(2)}, u32[]{:S(2)}) collective-permute-start(bf16[128,2048]{1,0:T(8,128)(2,1)S(1)} %copy-done.20), channel_id=1, source_target_pairs={{0,1},{1,0},{2,3},{3,2},{4,5},{5,4},{6,7},{7,6},{8,9},{9,8},{10,11... | collective-permute-start | bytes 1572872 | tf_op jit(solution)/shard_map/o2/ppermute | solution.py:375
  85.0 27.5 %collective-permute-start.14 = (bf16[128,4096]{1,0:T(8,128)(2,1)S(1)}, bf16[128,4096]{1,0:T(8,128)(2,1)S(1)}, u32[]{:S(2)}, u32[]{:S(2)}) collective-permute-start(bf16[128,4096]{1,0:T(8,128)(2,1)S(1)} %add_parts.7), channel_id=1, source_target_pairs={{0,2},{1,3},{6,4},{7,5},{8,10},{9,11},{14,12},{15,13},{16,18},{17,... | collective-permute-start | bytes 3145736 | tf_op jit(solution)/shard_map/ra2/ppermute | solution.py:379
  89.4 23.0 %collective-permute-start.11 = (bf16[128,4096]{1,0:T(8,128)(2,1)S(1)}, bf16[128,4096]{1,0:T(8,128)(2,1)S(1)}, u32[]{:S(2)}, u32[]{:S(2)}) collective-permute-start(bf16[128,4096]{1,0:T(8,128)(2,1)S(1)} %add_parts.6), channel_id=1, source_target_pairs={{2,4},{3,5},{4,2},{5,3},{10,12},{11,13},{12,10},{13,11},{18,20},{1... | collective-permute-start | bytes 3145736 | tf_op jit(solution)/shard_map/rb2/ppermute | solution.py:379
  90.2 13.7 %copy-start.5 = (bf16[128,4096]{1,0:T(8,128)(2,1)}, bf16[128,4096]{1,0:T(8,128)(2,1)S(1)}, u32[]{:S(2)}) copy-start(bf16[128,4096]{1,0:T(8,128)(2,1)S(1)} %collective-permute-done.18.refs_1_.refs_6_) | copy-start | bytes 3145732
  90.2 13.6 %copy-start.7 = (bf16[128,4096]{1,0:T(8,128)(2,1)}, bf16[128,4096]{1,0:T(8,128)(2,1)S(1)}, u32[]{:S(2)}) copy-start(bf16[128,4096]{1,0:T(8,128)(2,1)S(1)} %collective-permute-done.19.refs_3_.refs_8_) | copy-start | bytes 3145732
  106.2 15.3 %copy-start.1 = (bf16[128,4096]{1,0:T(8,128)(2,1)}, bf16[128,4096]{1,0:T(8,128)(2,1)S(1)}, u32[]{:S(2)}) copy-start(bf16[128,4096]{1,0:T(8,128)(2,1)S(1)} %broadcast_select_fusion.refs_0_.refs_9_) | copy-start | bytes 3145732
  106.2 15.9 %copy-start.21 = (bf16[128,2048]{1,0:T(8,128)(2,1)S(1)}, bf16[128,2048]{1,0:T(8,128)(2,1)}, u32[]{:S(2)}) copy-start(bf16[128,2048]{1,0:T(8,128)(2,1)} %get-tuple-element.147) | copy-start | bytes 1572868
  106.2 6.3 %collective-permute-start.20 = (bf16[128,4096]{1,0:T(8,128)(2,1)S(1)}, bf16[128,4096]{1,0:T(8,128)(2,1)S(1)}, u32[]{:S(2)}, u32[]{:S(2)}) collective-permute-start(bf16[128,4096]{1,0:T(8,128)(2,1)S(1)} %broadcast_select_fusion.refs_0_.refs_9_), channel_id=1, source_target_pairs={{0,1},{1,0},{2,3},{3,2},{4,5},{5,4},{6,7},{7,6},{8,9},{9,8},{10,11... | collective-permute-start | bytes 3145736 | tf_op jit(solution)/shard_map/h3/ppermute | solution.py:375
  112.4 9.1 %copy-start.8 = (bf16[128,4096]{1,0:T(8,128)(2,1)}, bf16[128,4096]{1,0:T(8,128)(2,1)S(1)}, u32[]{:S(2)}) copy-start(bf16[128,4096]{1,0:T(8,128)(2,1)S(1)} %collective-permute-done.20.refs_1_.refs_10_) | copy-start | bytes 3145732
  121.5 28.7 %collective-permute-start.21 = (bf16[256,2048]{1,0:T(8,128)(2,1)}, bf16[256,2048]{1,0:T(8,128)(2,1)S(1)}, u32[]{:S(2)}, u32[]{:S(2)}) collective-permute-start(bf16[256,2048]{1,0:T(8,128)(2,1)} %get-tuple-element.134), channel_id=1, source_target_pairs={{0,8},{8,0},{16,24},{24,16},{1,17},{9,25},{17,1},{25,9},{2,10},{10... | collective-permute-start | bytes 3145736 | tf_op jit(solution)/shard_map/f1/ppermute | solution.py:384
  122.1 1.3 copy-start.13
  122.1 28.9 %collective-permute-start.25 = (bf16[128,2048]{1,0:T(8,128)(2,1)S(1)}, bf16[128,2048]{1,0:T(8,128)(2,1)S(1)}, u32[]{:S(2)}, u32[]{:S(2)}) collective-permute-start(bf16[128,2048]{1,0:T(8,128)(2,1)S(1)} %copy-done.21), channel_id=1, source_target_pairs={{0,1},{1,0},{2,3},{3,2},{4,5},{5,4},{6,7},{7,6},{8,9},{9,8},{10,11... | collective-permute-start | bytes 1572872 | tf_op jit(solution)/shard_map/o3/ppermute | solution.py:375
  122.5 41.8 %collective-permute-start.23 = (bf16[128,4096]{1,0:T(8,128)(2,1)S(1)}, bf16[128,4096]{1,0:T(8,128)(2,1)S(1)}, u32[]{:S(2)}, u32[]{:S(2)}) collective-permute-start(bf16[128,4096]{1,0:T(8,128)(2,1)S(1)} %add_parts.9), channel_id=1, source_target_pairs={{2,4},{3,5},{4,2},{5,3},{10,12},{11,13},{12,10},{13,11},{18,20},{1... | collective-permute-start | bytes 3145736 | tf_op jit(solution)/shard_map/rb3/ppermute | solution.py:379
  123.4 7.5 %copy-start.18 = (bf16[256,2048]{1,0:T(8,128)(2,1)S(1)}, bf16[256,2048]{1,0:T(8,128)(2,1)}, u32[]{:S(2)}) copy-start(bf16[256,2048]{1,0:T(8,128)(2,1)} %get-tuple-element.146) | copy-start | bytes 3145732
  123.8 40.5 %collective-permute-start.22 = (bf16[128,4096]{1,0:T(8,128)(2,1)S(1)}, bf16[128,4096]{1,0:T(8,128)(2,1)S(1)}, u32[]{:S(2)}, u32[]{:S(2)}) collective-permute-start(bf16[128,4096]{1,0:T(8,128)(2,1)S(1)} %add_parts.8), channel_id=1, source_target_pairs={{0,2},{1,3},{2,0},{3,1},{4,6},{5,7},{6,4},{7,5},{8,10},{9,11},{10,... | collective-permute-start | bytes 3145736 | tf_op jit(solution)/shard_map/ra3/ppermute | solution.py:379
  130.9 19.3 %copy-start.6 = (bf16[256,2048]{1,0:T(8,128)(2,1)S(1)}, bf16[256,2048]{1,0:T(8,128)(2,1)}, u32[]{:S(2)}) copy-start(bf16[256,2048]{1,0:T(8,128)(2,1)} %get-tuple-element.133.a) | copy-start | bytes 3145732
  130.9 33.4 %collective-permute-start.24 = (bf16[256,2048]{1,0:T(8,128)(2,1)S(1)}, bf16[256,2048]{1,0:T(8,128)(2,1)S(1)}, u32[]{:S(2)}, u32[]{:S(2)}) collective-permute-start(bf16[256,2048]{1,0:T(8,128)(2,1)S(1)} %copy-done.18), channel_id=1, source_target_pairs={{0,8},{8,0},{16,24},{24,16},{1,17},{9,25},{17,1},{25,9},{2,10},{10... | collective-permute-start | bytes 3145736 | tf_op jit(solution)/shard_map/e1/ppermute | solution.py:384
  150.2 1.0 copy-start.22
  150.2 1.0 copy-start.23
  150.4 15.6 %collective-permute-start.27 = (bf16[256,2048]{1,0:T(8,128)(2,1)S(1)}, bf16[256,2048]{1,0:T(8,128)(2,1)S(1)}, u32[]{:S(2)}, u32[]{:S(2)}) collective-permute-start(bf16[256,2048]{1,0:T(8,128)(2,1)S(1)} %add_pair.1), channel_id=1, source_target_pairs={{0,16},{8,24},{16,0},{24,8},{1,9},{9,1},{17,25},{25,17},{2,18},{10... | collective-permute-start | bytes 3145736 | tf_op jit(solution)/shard_map/e2/ppermute | solution.py:384
  151.2 13.1 %collective-permute-start.26 = (bf16[128,2048]{1,0:T(8,128)(2,1)S(1)}, bf16[128,2048]{1,0:T(8,128)(2,1)S(1)}, u32[]{:S(2)}, u32[]{:S(2)}) collective-permute-start(bf16[128,2048]{1,0:T(8,128)(2,1)S(1)} %copy-done.22), channel_id=1, source_target_pairs={{0,1},{1,0},{2,3},{3,2},{4,5},{5,4},{6,7},{7,6},{8,9},{9,8},{10,11... | collective-permute-start | bytes 1572872 | tf_op jit(solution)/shard_map/o3/ppermute | solution.py:375
  151.2 13.1 %copy-start.12 = (bf16[128,4096]{1,0:T(8,128)(2,1)S(1)}, bf16[128,4096]{1,0:T(8,128)(2,1)}, u32[]{:S(2)}) copy-start(bf16[128,4096]{1,0:T(8,128)(2,1)} %grad.1) | copy-start | bytes 3145732
  151.2 13.1 %copy-start.14 = (bf16[128,4096]{1,0:T(8,128)(2,1)S(1)}, bf16[128,4096]{1,0:T(8,128)(2,1)}, u32[]{:S(2)}) copy-start(bf16[128,4096]{1,0:T(8,128)(2,1)} %get-tuple-element.145.q) | copy-start | bytes 3145732
  164.4 1.7 %copy-start.17 = (bf16[256,2048]{1,0:T(8,128)(2,1)S(1)}, bf16[256,2048]{1,0:T(8,128)(2,1)}, u32[]{:S(2)}) copy-start(bf16[256,2048]{1,0:T(8,128)(2,1)} %get-tuple-element.153) | copy-start | bytes 3145732
